TPU v7x, 512 devices: a whole 4x8x8 slice. The times are simulated.
512 devices in a mesh: section: 16 (over z, x_hi), dp: 32 (over y, x_lo, core).
Axes of the slice: x: 4 (x_hi: 2, x_lo: 2; x = x_hi * 2 + x_lo), y: 8, z: 8, core: 2. Of those that a mesh axis runs over, the one named last changes fastest.
Arguments:
- acts: bfloat16 [16, 4096, 8192], P('section', 'dp'), may hold values from -1000 to 1000
- gain: float32 [16, 8192], P('section'), may hold values from 0.1 to 1.9
- kv_grad: bfloat16 [16, 4096, 256], P('section', 'dp'), may hold values from -6 to 6
- master: float32 [16, 8192, 256], P('section', 'dp'), may hold values from -0.0625 to 0.0625
- moment_one: float32 [16, 8192, 256], P('section', 'dp'), may hold values from -320 to 320
- moment_two: float32 [16, 8192, 256], P('section', 'dp'), may hold values from 1000 to 1000000
Outputs:
- new_master: float32 [16, 8192, 256], P('section', 'dp')
- new_moment_one: float32 [16, 8192, 256], P('section', 'dp')
- new_moment_two: float32 [16, 8192, 256], P('section', 'dp')
- input_grad: bfloat16 [4096, 8192], P('dp', 'section')
- kv_next: float32 [16, 4096, 256], P('section', 'dp')
All inputs are finite; a program needn't handle non-finite values.
Results may differ from a plain program's by a relative error of at most 0.0049.
The roundings to bfloat16 on the way count: a program that leaves them out, or rounds other values in their place, can miss the bound.
Values may be sent and summed in bfloat16 or wider, within the bound.
A program may use at most 64 MiB of HBM per device.

v0:
```python
import jax
import jax.numpy as jnp
from jax import lax
from jax.sharding import PartitionSpec as P

STEP = 20


NORM_EPS = 1e-05
ADAM_EPS = 1e-08
BETA_ONE = 0.9
BETA_TWO = 0.95
LEARN_RATE = 0.00015
DECAY_RATE = 0.1


def normed(inputs, gain_row):
    values = inputs.astype(jnp.float32)
    root_mean = jnp.sqrt(jnp.mean(values * values, axis=-1, keepdims=True) + NORM_EPS)
    unit_rows = values / root_mean
    return (root_mean, unit_rows, (unit_rows * gain_row).astype(jnp.bfloat16))


def per_device(acts, gain, kv_grad, master, moment_one, moment_two):
    gain_row = gain[0]
    upstream = kv_grad[0]
    owned_rows = master[0]
    root_mean, unit_rows, hidden = normed(acts[0], gain_row)
    token_count = hidden.shape[0]
    feature_count = hidden.shape[1]
    section_count = lax.axis_size("section")
    back_proj = lax.dot_general(
        upstream,
        lax.all_gather(owned_rows.astype(jnp.bfloat16), "dp", axis=0, tiled=True),
        (((1,), (1,)), ((), ())),
        preferred_element_type=jnp.float32,
    )
    scaled = back_proj * gain_row
    branch_grad = (
        (scaled - unit_rows * jnp.mean(scaled * unit_rows, axis=-1, keepdims=True)) / root_mean
    ).astype(jnp.bfloat16)
    column_blocks = branch_grad.reshape(token_count, section_count, feature_count // section_count)
    received = lax.all_to_all(column_blocks, "section", split_axis=1, concat_axis=1, tiled=True)
    input_grad = jnp.sum(received, axis=1, dtype=jnp.float32).astype(jnp.bfloat16)
    gradient = lax.psum_scatter(
        lax.dot_general(
            hidden, upstream, (((0,), (0,)), ((), ())), preferred_element_type=jnp.float32
        ).astype(jnp.bfloat16),
        "dp",
        scatter_dimension=0,
        tiled=True,
    ).astype(jnp.float32)
    first_new = BETA_ONE * moment_one[0] + (1.0 - BETA_ONE) * gradient
    second_new = BETA_TWO * moment_two[0] + (1.0 - BETA_TWO) * gradient * gradient
    direction = (
        first_new
        / (1.0 - BETA_ONE**STEP)
        / (jnp.sqrt(second_new / (1.0 - BETA_TWO**STEP)) + ADAM_EPS)
    )
    updated = owned_rows - LEARN_RATE * (direction + DECAY_RATE * owned_rows)
    fresh_part = updated.astype(jnp.bfloat16)
    weight_new = lax.all_gather(fresh_part, "dp", axis=0, tiled=True)
    kv_next = jnp.dot(hidden, weight_new, preferred_element_type=jnp.float32)
    return (updated[None], first_new[None], second_new[None], input_grad, kv_next[None])


def solution(mesh):
    placed = (
        P("section", "dp", None),
        P("section", None),
        P("section", "dp", None),
        P("section", "dp", None),
        P("section", "dp", None),
        P("section", "dp", None),
    )
    return jax.shard_map(
        per_device,
        mesh=mesh,
        in_specs=placed,
        out_specs=(
            P("section", "dp", None),
            P("section", "dp", None),
            P("section", "dp", None),
            P("dp", "section"),
            P("section", "dp", None),
        ),
        check_vma=False,
    )
```

profile of v0, /device:TPU:1, one launch (start us, length us, event | category | flops | bytes accessed | tf_op | source)
XLA Modules:
  0.0 299.9 jit_solution(17889752518784754334)
XLA Ops:
  7.2 0.0 copy-start
  7.2 0.0 reduce-scatter.2.cloned.1.call-start
  7.2 2.1 fusion.2
  9.3 5.0 %convolution_convert_fusion = bf16[8192,256]{1,0:T(8,128)(2,1)} fusion(bf16[1,128,8192]{2,1,0:T(8,128)(2,1)} %param.6, f32[8192]{0:T(1024)} %bitcast.67, f32[128]{0:T(128)S(1)} %add_sqrt_fusion, bf16[1,128,256]{2,1,0:T(8,128)(2,1)S(1)} %copy-done), kind=kOutput, calls=%fused_computation | convolution fusion | flops 543162368 | bytes 6390272 | tf_op jit(solution)/shard_map/dot_general | solution.py:46
  14.3 0.0 copy-start.5
  14.3 0.0 reduce-scatter.2.cloned.1.call-update
  14.4 0.0 all-gather.3.cloned.1.call-start
  14.4 0.8 copy-done.2
  15.3 0.7 bitcast_convert_fusion
  15.9 0.0 all-gather.3.cloned.1.call-update
  16.0 0.0 all-gather.5.cloned.1.call-start
  16.0 127.1 %reduce-scatter.2.cloned.1.call-done = bf16[256,256]{1,0:T(8,128)(2,1)} async-done(((bf16[8192,256]{1,0:T(8,128)(2,1)}), bf16[256,256]{1,0:T(8,128)(2,1)}) %reduce-scatter.2.cloned.1.call-update) | async-done | bytes 131088 | tf_op jit(solution)/shard_map/reduce_scatter | solution.py:45
  143.1 0.0 copy-done.4
  143.1 2.0 fusion.21
  145.1 0.0 all-gather.5.cloned.1.call-update
  145.1 71.3 %all-gather.3.cloned.1.call-done = bf16[8192,256]{1,0:T(8,128)(2,1)} async-done(((bf16[256,256]{1,0:T(8,128)(2,1)}), bf16[8192,256]{1,0:T(8,128)(2,1)}) %all-gather.3.cloned.1.call-update) | async-done | bytes 4194320 | tf_op jit(solution)/shard_map/all_gather | solution.py:34
  216.4 0.0 copy-done.1
  216.4 3.8 %multiply_reduce_fusion = (f32[128]{0:T(128)S(1)}, f32[128,8192]{1,0:T(8,128)S(1)}) fusion(f32[128]{0:T(128)S(1)} %add_sqrt_fusion, bf16[1,128,8192]{2,1,0:T(8,128)(2,1)S(1)} %copy-done.1, f32[8192]{0:T(1024)S(1)} %bitcast.68, bf16[8192,256]{1,0:T(8,128)(2,1)} %all-gather.3.cloned.1.call-done, bf16[1,128,256]{2,1,0:T(8,128)(2,1)S(1)} %copy-done), kind=kOutput, calls=%fused_computation.11 | convolution fusion | flops 542113664 | bytes 10585088 | tf_op jit(solution)/shard_map/dot_general | solution.py:32
  220.2 0.9 divide_convert_fusion
  221.1 0.2 copy.14
  221.3 60.8 %all_to_all.5 = bf16[128,16,512]{2,0,1:T(8,128)(2,1)} all-to-all(bf16[128,16,512]{2,0,1:T(8,128)(2,1)S(1)} %bitcast.65), channel_id=1, replica_groups=mesh['section'=16,'dp'=32] {'section'}, dimensions={1} | all-to-all | bytes 4194304 | tf_op jit(solution)/shard_map/all_to_all | solution.py:43
  282.2 2.6 reduce_sum.32
  284.8 5.0 %all-gather.5.cloned.1.call-done = bf16[8192,256]{1,0:T(8,128)(2,1)} async-done(((bf16[256,256]{1,0:T(8,128)(2,1)}), bf16[8192,256]{1,0:T(8,128)(2,1)}) %all-gather.5.cloned.1.call-update) | async-done | bytes 4194320 | tf_op jit(solution)/shard_map/all_gather | solution.py:62
  289.7 3.7 %fusion.11 = f32[1,128,256]{2,1,0:T(8,128)} fusion(bf16[8192,256]{1,0:T(8,128)(2,1)} %all-gather.5.cloned.1.call-done, f32[8192]{0:T(1024)S(1)} %bitcast.69, bf16[1,128,8192]{2,1,0:T(8,128)(2,1)S(1)} %copy-done.1, f32[128]{0:T(128)S(1)} %add_sqrt_fusion), kind=kOutput, calls=%fused_computation.18 | convolution fusion | flops 541065216 | bytes 6455808 | tf_op jit(solution)/shard_map/dot_general | solution.py:63
  (9 shorter events, 0.0 us)
Async XLA Ops:
  7.2 2.2 copy-start
  7.2 135.9 %reduce-scatter.2.cloned.1.call-start = ((), (), s32[]{:S(2)}) async-start(), calls=%async_computation.2 | async-start | bytes 4325376 | tf_op jit(solution)/shard_map/reduce_scatter | solution.py:45
  14.3 0.9 copy-start.2
  14.3 128.7 %copy-start.3 = (f32[1,256,256]{2,1,0:T(8,128)S(1)}, f32[1,256,256]{2,1,0:T(8,128)}, u32[]{:S(2)}) copy-start(f32[1,256,256]{2,1,0:T(8,128)} %param.11) | copy-start | bytes 786436
  14.3 128.7 %copy-start.4 = (f32[1,256,256]{2,1,0:T(8,128)S(1)}, f32[1,256,256]{2,1,0:T(8,128)}, u32[]{:S(2)}) copy-start(f32[1,256,256]{2,1,0:T(8,128)} %param.10) | copy-start | bytes 786436
  14.3 202.1 %copy-start.1 = (bf16[1,128,8192]{2,1,0:T(8,128)(2,1)S(1)}, bf16[1,128,8192]{2,1,0:T(8,128)(2,1)}, u32[]{:S(2)}) copy-start(bf16[1,128,8192]{2,1,0:T(8,128)(2,1)} %param.6) | copy-start | bytes 6291460
  14.3 202.1 %copy-start.5 = (f32[1,8192]{1,0:T(1,128)S(1)}, f32[1,8192]{1,0:T(1,128)}, u32[]{:S(2)}) copy-start(f32[1,8192]{1,0:T(1,128)} %param.7) | copy-start | bytes 98308
  14.4 202.0 %all-gather.3.cloned.1.call-start = ((), (), s32[]{:S(2)}) async-start(), calls=%async_computation.3 | async-start | bytes 4325376 | tf_op jit(solution)/shard_map/all_gather | solution.py:34
  16.0 273.8 %all-gather.5.cloned.1.call-start = ((), (), s32[]{:S(2)}) async-start(), calls=%async_computation.4 | async-start | bytes 4325376 | tf_op jit(solution)/shard_map/all_gather | solution.py:62
Sparse Core Ops, SparseCore 0:
  14.5 128.5 reduce-scatter.1
  145.8 70.5 all-gather.2
  219.1 70.5 all-gather.4
where the time goes:
time: 300 us
  waiting for transfers between devices  203 us (68%)
  blocking collectives  60.8 us (20%)
  between operations  13.8 us (5%)
  matrix products  12.5 us (4%)
  other arithmetic  8.26 us (3%)
    reduce_scatter x1, waiting for transfers between devices, per_device(): lax.psum_scatter(lax.dot_general(hidden, upstream, (((0,), (0,)), ((), ()...  127 us
    all_gather x1, waiting for transfers between devices, per_device(): lax.all_gather(owned_rows.astype(jnp.bfloat16), 'dp', axis=0, tiled=True)  71.3 us
    all_to_all x1, blocking collectives, per_device(): lax.all_to_all(column_blocks, 'section', split_axis=1, concat_axis=1, til...  60.8 us
  transfers between devices with their start and end apart: 3, of which 3 were waited for; matrix products, arithmetic and copies ran while one was open for 3% of the time, Pallas kernels for 0%

commit v1 on v0

v1 whole, which is shorter than its diff:
```python
import jax
import jax.numpy as jnp
from jax import lax
from jax.experimental import pallas as pl
from jax.experimental.pallas import tpu as pltpu
from jax.sharding import PartitionSpec as P

STEP = 20
NORM_EPS = 1e-05
ADAM_EPS = 1e-08
BETA_ONE = 0.9
BETA_TWO = 0.95
LEARN_RATE = 0.00015
DECAY_RATE = 0.1

F32 = jnp.float32
BF16 = jnp.bfloat16
N = 8
D = 8192
TOK = 128
HALF = 64
W = 256
GATHER_ORDER = (0, 1, 7, 2, 6, 3, 5, 4)
SCATTER_ORDER = (4, 3, 5, 2, 6, 1, 7, 0)


def rows_of(half):
    return pl.ds(half * HALF, HALF)


def wide(a):
    return jnp.concatenate([a, a], axis=-1)


def kernel(
    acts, gain, kv, master, mom1, mom2,
    o_master, o_m1, o_m2, o_in, o_kv,
    a_full, gain_v, mas_v, m1_v, m2_v,
    xa, kvb, kvt, rmb, invc, wt, wn, hid, sc, macc, msend, mrecv, mcol,
    gfin, ysend, yrecv, zsend, zrecv, xsend, xrecv, kvn, knr,
    nm_v, n1_v, n2_v, oin_v, okv_v,
    l_in, l_acts, s_acts, r_acts, s_kv, r_kv, s_rm, r_rm, s_m, r_m,
    s_w, r_w, s_n, r_n, s_y, r_y, s_z, r_z, s_x, r_x, s_k, r_k, l_out,
):
    section = lax.axis_index("section")
    dp = lax.axis_index("dp")
    z = lax.div(section, 2)
    xh = lax.rem(section, 2)
    y = lax.div(dp, 4)
    q = lax.rem(dp, 4)
    xl = lax.div(q, 2)
    c = lax.rem(q, 2)
    mates = (xl * 2 + (1 - c), (1 - xl) * 2 + c, (1 - xl) * 2 + (1 - c))

    def ring(at, off):
        return lax.rem(at + off, N)

    def y_dev(off):
        return (section, ring(y, off) * 4 + q)

    def z_dev(off):
        return (ring(z, off) * 2 + xh, dp)

    def mate_dev(mate):
        return (section, y * 4 + mate)

    def remote(src, dst, send, recv, device):
        return pltpu.make_async_remote_copy(
            src_ref=src, dst_ref=dst, send_sem=send, recv_sem=recv,
            device_id=device, device_id_type=pl.DeviceIdType.MESH,
        )

    def wait_bytes(ref, sem):
        pltpu.make_async_copy(ref, ref, sem).wait()

    def columns(block):
        return pl.ds(pl.multiple_of(block * 1024 + q * W, W), W)

    loads = [
        pltpu.make_async_copy(master.at[0], mas_v, l_in.at[0]),
        pltpu.make_async_copy(acts.at[0], a_full, l_in.at[1]),
        pltpu.make_async_copy(kv.at[0], kvb.at[q], l_in.at[2]),
        pltpu.make_async_copy(gain, gain_v, l_in.at[3]),
        pltpu.make_async_copy(mom1.at[0], m1_v, l_in.at[4]),
        pltpu.make_async_copy(mom2.at[0], m2_v, l_in.at[5]),
    ]
    for load in loads:
        load.start()

    def own_acts(i):
        block = ring(y, GATHER_ORDER[i])
        return pltpu.make_async_copy(acts.at[0, :, columns(block)], xa.at[block, q], l_acts.at[i])

    for i in range(N):
        own_acts(i).start()

    barrier = pltpu.get_barrier_semaphore()
    for fh in range(2):
        for fl in range(2):
            for fc in range(2):
                if fh + fl + fc == 0:
                    continue
                other_h = 1 - xh if fh else xh
                other_l = 1 - xl if fl else xl
                other_c = 1 - c if fc else c
                pl.semaphore_signal(
                    barrier, inc=1, device_id=(z * 2 + other_h, y * 4 + other_l * 2 + other_c),
                    device_id_type=pl.DeviceIdType.MESH,
                )
    for device in (y_dev(1), y_dev(7), z_dev(1), z_dev(7)):
        pl.semaphore_signal(barrier, inc=1, device_id=device, device_id_type=pl.DeviceIdType.MESH)
    pl.semaphore_wait(barrier, 11)

    def send_acts(half, i):
        order = (GATHER_ORDER, SCATTER_ORDER)[half]
        block = ring(y, order[i])
        for mate in mates:
            source = acts.at[0, rows_of(half), pl.ds(pl.multiple_of(block * 1024 + mate * W, W), W)]
            remote(source, xa.at[block, q, rows_of(half)], s_acts.at[half, i], r_acts.at[half, i], mate_dev(mate)).start()

    def wait_acts(half, i):
        if half == 0:
            own_acts(i).wait()
        wait_bytes(xa.at[0, pl.ds(0, 3), rows_of(0)], r_acts.at[half, i])

    for mate in mates:
        remote(kv.at[0], kvb.at[q], s_kv, r_kv, mate_dev(mate)).start()
    send_acts(0, 0)
    send_acts(0, 1)

    def gather_copy(buffer, send, recv, way, hop):
        off = N - hop if way == 0 else hop
        block = buffer.at[ring(y, off)]
        if hop == 3:
            block = block.at[pl.ds(way * 128, 128)]
        return remote(block, block, send.at[way, hop], recv.at[way, hop], y_dev(1 if way == 0 else 7))

    def gather_hop(buffer, send, recv, hop):
        for way in range(2):
            if hop > 0:
                gather_copy(buffer, send, recv, way, hop - 1).wait_recv()
            if hop < 4:
                gather_copy(buffer, send, recv, way, hop).start()

    loads[0].wait()
    wt[y] = jnp.transpose(mas_v[...]).astype(BF16)
    gather_hop(wt, s_w, r_w, 0)

    loads[1].wait()

    def add_squares(step, total):
        part = a_full[:, pl.ds(pl.multiple_of(step * 512, 512), 512)].astype(F32)
        part = part * part
        return total + ((part[:, :128] + part[:, 128:256]) + (part[:, 256:384] + part[:, 384:]))

    squares = lax.fori_loop(0, 16, add_squares, jnp.zeros((TOK, 128), F32))
    mean_row = jnp.sum(jnp.transpose(squares), axis=0, keepdims=True) / D
    rmb[q] = jnp.broadcast_to(jnp.sqrt(mean_row + NORM_EPS), (8, 128))
    for mate in mates:
        remote(rmb.at[q], rmb.at[q], s_rm, r_rm, mate_dev(mate)).start()
    for i in range(2, N):
        send_acts(0, i)

    for load in loads[2:4]:
        load.wait()
    wait_bytes(kvb.at[pl.ds(0, 3)], r_kv)
    wait_bytes(rmb.at[pl.ds(0, 3)], r_rm)

    def prepare(slot, carry):
        root = jnp.transpose(jnp.broadcast_to(rmb[slot][0:1, :], (128, 128)))
        invc[slot] = 1.0 / root
        kvt[slot] = jnp.transpose(kvb[slot].astype(F32)).astype(BF16)
        return carry

    lax.fori_loop(0, 4, prepare, 0)

    def forward(half, block):
        gain_row = gain_v[:, columns(block)]
        back = jnp.dot(
            kvb[:, rows_of(half), :].reshape(4 * HALF, W), wt[block], preferred_element_type=F32
        )
        sc[block, :, rows_of(half), :] = back.reshape(4, HALF, W)

        def one(slot, carry):
            unit = xa[block, slot, rows_of(half), :].astype(F32) * wide(invc[slot, rows_of(half), :])
            hid[block, slot, rows_of(half), :] = (unit * gain_row).astype(BF16)
            scaled = sc[block, slot, rows_of(half), :] * gain_row
            sc[block, slot, rows_of(half), :] = scaled
            product = scaled * unit
            macc[half, slot] += product[:, :128] + product[:, 128:]
            return carry

        lax.fori_loop(0, 4, one, 0)

    def send_means(half):
        msend[half] = jnp.zeros((8, 128), F32)
        for pair in range(2):
            both = macc[half, pl.ds(pair * 2, 2)].reshape(128, 128)
            msend[half, pair : pair + 1, :] = jnp.sum(jnp.transpose(both), axis=0, keepdims=True)
        for r, mate in enumerate(mates):
            remote(msend.at[half], mrecv.at[half, r], s_m.at[half, r], r_m.at[half, r], mate_dev(mate)).start()

    def get_means(half):
        for r, mate in enumerate(mates):
            remote(msend.at[half], mrecv.at[half, r], s_m.at[half, r], r_m.at[half, r], mate_dev(mate)).wait_recv()
        total = ((msend[half] + mrecv[half, 0]) + (mrecv[half, 1] + mrecv[half, 2])) / D
        for pair in range(2):
            column = jnp.transpose(jnp.broadcast_to(total[pair : pair + 1, :], (128, 128)))
            mcol[half, pl.ds(pair * 2, 2)] = column.reshape(2, HALF, 128)

    def branch(half, block, slot):
        inv = wide(invc[slot, rows_of(half), :])
        unit = xa[block, slot, rows_of(half), :].astype(F32) * inv
        return ((sc[block, slot, rows_of(half), :] - unit * wide(mcol[half, slot])) * inv).astype(BF16)

    def z_copy(half, way, step):
        part = pl.ds(2 * way, 2) if step == 0 else pl.ds(0, 4)
        return remote(
            zsend.at[half, way, step, part], zrecv.at[half, way, step, part],
            s_z.at[half, way, step], r_z.at[half, way, step], z_dev(1 if way == 0 else 7),
        )

    def z_step(half, step):
        if step == 0:
            block = ring(z, 4)
            for way in range(2):
                for slot in (2 * way, 2 * way + 1):
                    zsend[half, way, 0, slot] = branch(half, block, slot)
                z_copy(half, way, 0).start()
            return
        for way in range(2):
            z_copy(half, way, step - 1).wait_recv()
            block = ring(z, 4 - step if way == 0 else 4 + step)

            def one(slot, carry):
                own = branch(half, block, slot).astype(F32)
                zsend[half, way, step, slot] = (own + zrecv[half, way, step - 1, slot].astype(F32)).astype(BF16)
                return carry

            if step == 1:
                for slot in range(4):
                    if slot // 2 == way:
                        one(slot, 0)
                    else:
                        zsend[half, way, step, slot] = branch(half, block, slot)
            else:
                lax.fori_loop(0, 4, one, 0)
            z_copy(half, way, step).start()

    x_section = z * 2 + xl
    x_source = xh * 2 + c

    def x_copy(half, slot):
        return remote(
            xsend.at[half, slot], xrecv.at[half, x_source], s_x.at[half, slot], r_x.at[half, x_source],
            (x_section, y * 4 + slot),
        )

    def stays(slot):
        return jnp.logical_and(xh == xl, q == slot)

    def z_last(half):
        for way in range(2):
            z_copy(half, way, 3).wait_recv()

        def one(slot, carry):
            total = branch(half, z, slot).astype(F32)
            total = total + (zrecv[half, 0, 3, slot].astype(F32) + zrecv[half, 1, 3, slot].astype(F32))
            xsend[half, slot] = total.astype(BF16)
            return carry

        lax.fori_loop(0, 4, one, 0)
        for slot in range(4):
            @pl.when(stays(slot))
            def _():
                pltpu.make_async_copy(xsend.at[half, slot], xrecv.at[half, x_source], r_x.at[half, x_source]).start()

            @pl.when(jnp.logical_not(stays(slot)))
            def _():
                x_copy(half, slot).start()

    def x_last(half):
        for source in range(4):
            wait_bytes(xrecv.at[half, source], r_x.at[half, source])
        for col in range(2):
            total = xrecv[half, col].astype(F32) + xrecv[half, 2 + col].astype(F32)
            oin_v[rows_of(half), col * W : (col + 1) * W] = total.astype(BF16)

    macc[...] = jnp.zeros_like(macc)
    for i in range(N):
        send_acts(1, i)
        if i in (1, 3, 5, 7):
            gather_hop(wt, s_w, r_w, (i + 1) // 2)
        wait_acts(0, i)
        forward(0, ring(y, GATHER_ORDER[i]))
    send_means(0)

    def y_copy(way, step):
        part = pl.ds(way * 128, 128) if step == 0 else pl.ds(0, W)
        return remote(
            ysend.at[way, step, part], yrecv.at[way, step, part], s_y.at[way, step], r_y.at[way, step],
            y_dev(1 if way == 0 else 7),
        )

    for i in range(N):
        if i == 0:
            get_means(0)
        if i % 2 == 0:
            z_step(0, i // 2)
        off = SCATTER_ORDER[i]
        block = ring(y, off)
        wait_acts(1, i)
        forward(1, block)
        total = None
        for slot in range(4):
            product = jnp.dot(kvt[slot], hid[block, slot], preferred_element_type=F32).astype(BF16).astype(F32)
            total = product if total is None else total + product
        if off == 4:
            ysend[0, 0] = total.astype(BF16)
            ysend[1, 0] = total.astype(BF16)
            for way in range(2):
                y_copy(way, 0).start()
        elif off == 0:
            for way in range(2):
                y_copy(way, 3).wait_recv()
            gfin[...] = total + (yrecv[0, 3].astype(F32) + yrecv[1, 3].astype(F32))
        else:
            way = 0 if off < 4 else 1
            step = 4 - off if off < 4 else off - 4
            y_copy(way, step - 1).wait_recv()
            got = yrecv[way, step - 1]
            if step == 1:
                ysend[way, 1] = total.astype(BF16)
                mine = slice(way * 128, way * 128 + 128)
                ysend[way, 1, mine, :] = (total[mine] + got[mine].astype(F32)).astype(BF16)
            else:
                ysend[way, step] = (total + got.astype(F32)).astype(BF16)
            y_copy(way, step).start()
    send_means(1)

    for load in loads[4:6]:
        load.wait()
    gradient = jnp.transpose(gfin[...])
    old = mas_v[...]
    first_new = BETA_ONE * m1_v[...] + (1.0 - BETA_ONE) * gradient
    second_new = BETA_TWO * m2_v[...] + (1.0 - BETA_TWO) * gradient * gradient
    direction = (
        first_new / (1.0 - BETA_ONE**STEP) / (jnp.sqrt(second_new / (1.0 - BETA_TWO**STEP)) + ADAM_EPS)
    )
    updated = old - LEARN_RATE * (direction + DECAY_RATE * old)
    wn[y] = updated.astype(BF16)
    gather_hop(wn, s_n, r_n, 0)
    nm_v[...] = updated
    n1_v[...] = first_new
    n2_v[...] = second_new
    stores = [
        pltpu.make_async_copy(nm_v, o_master.at[0], l_out.at[0]),
        pltpu.make_async_copy(n1_v, o_m1.at[0], l_out.at[1]),
        pltpu.make_async_copy(n2_v, o_m2.at[0], l_out.at[2]),
    ]
    for store in stores:
        store.start()

    def next_part(off, first=False):
        block = ring(y, off)
        part = jnp.dot(hid[block].reshape(4 * TOK, W), wn[block], preferred_element_type=F32).reshape(4, TOK, W)
        kvn[...] = part if first else kvn[...] + part

    z_last(0)
    get_means(1)
    z_step(1, 0)
    next_part(0, True)
    gather_hop(wn, s_n, r_n, 1)
    z_step(1, 1)
    next_part(1)
    next_part(7)
    gather_hop(wn, s_n, r_n, 2)
    x_last(0)
    next_part(2)
    next_part(6)
    z_step(1, 2)
    gather_hop(wn, s_n, r_n, 3)
    next_part(3)
    next_part(5)
    gather_hop(wn, s_n, r_n, 4)
    next_part(4)

    def next_copy(r, mate):
        return remote(kvn.at[mate], knr.at[r], s_k.at[r], r_k.at[r], mate_dev(mate))

    for r, mate in enumerate(mates):
        next_copy(r, mate).start()
    z_step(1, 3)
    for r, mate in enumerate(mates):
        next_copy(r, mate).wait_recv()
    okv_v[...] = (kvn[q] + knr[0]) + (knr[1] + knr[2])
    stores.append(pltpu.make_async_copy(okv_v, o_kv.at[0], l_out.at[3]))
    stores[-1].start()
    z_last(1)
    x_last(1)
    stores.append(pltpu.make_async_copy(oin_v, o_in, l_out.at[4]))
    stores[-1].start()

    wait_bytes(kvb.at[pl.ds(0, 3)], s_kv)
    wait_bytes(rmb.at[pl.ds(0, 3)], s_rm)
    for half in range(2):
        for i in range(N):
            wait_bytes(xa.at[0, pl.ds(0, 3), rows_of(0)], s_acts.at[half, i])
        for r, mate in enumerate(mates):
            remote(msend.at[half], mrecv.at[half, r], s_m.at[half, r], r_m.at[half, r], mate_dev(mate)).wait_send()
        for way in range(2):
            for step in range(4):
                z_copy(half, way, step).wait_send()
        for slot in range(4):
            @pl.when(jnp.logical_not(stays(slot)))
            def _():
                x_copy(half, slot).wait_send()
    for way in range(2):
        for step in range(4):
            gather_copy(wt, s_w, r_w, way, step).wait_send()
            gather_copy(wn, s_n, r_n, way, step).wait_send()
            y_copy(way, step).wait_send()
    for r, mate in enumerate(mates):
        next_copy(r, mate).wait_send()
    for store in stores:
        store.wait()


def per_device(acts, gain, kv_grad, master, moment_one, moment_two):
    anywhere = pl.BlockSpec(memory_space=pl.ANY)
    vmem = pltpu.VMEM
    dma = pltpu.SemaphoreType.DMA
    rows = jax.ShapeDtypeStruct((1, W, W), F32)
    scratch = [
        vmem((TOK, D), BF16),
        vmem((1, D), F32),
        vmem((W, W), F32), vmem((W, W), F32), vmem((W, W), F32),
        vmem((N, 4, TOK, W), BF16),
        vmem((4, TOK, W), BF16),
        vmem((4, W, TOK), BF16),
        vmem((4, 8, 128), F32),
        vmem((4, TOK, 128), F32),
        vmem((N, W, W), BF16),
        vmem((N, W, W), BF16),
        vmem((N, 4, TOK, W), BF16),
        vmem((N, 4, TOK, W), F32),
        vmem((2, 4, HALF, 128), F32),
        vmem((2, 8, 128), F32),
        vmem((2, 3, 8, 128), F32),
        vmem((2, 4, HALF, 128), F32),
        vmem((W, W), F32),
        vmem((2, 4, W, W), BF16), vmem((2, 4, W, W), BF16),
        vmem((2, 2, 4, 4, HALF, W), BF16), vmem((2, 2, 4, 4, HALF, W), BF16),
        vmem((2, 4, HALF, W), BF16), vmem((2, 4, HALF, W), BF16),
        vmem((4, TOK, W), F32),
        vmem((3, TOK, W), F32),
        vmem((W, W), F32), vmem((W, W), F32), vmem((W, W), F32),
        vmem((TOK, 2 * W), BF16),
        vmem((TOK, W), F32),
        dma((6,)), dma((N,)), dma((2, N)), dma((2, N)),
        dma, dma, dma, dma,
        dma((2, 3)), dma((2, 3)),
        dma((2, 4)), dma((2, 4)), dma((2, 4)), dma((2, 4)),
        dma((2, 4)), dma((2, 4)),
        dma((2, 2, 4)), dma((2, 2, 4)),
        dma((2, 4)), dma((2, 4)),
        dma((3,)), dma((3,)), dma((5,)),
    ]
    return pl.pallas_call(
        kernel,
        out_shape=(
            rows, rows, rows,
            jax.ShapeDtypeStruct((TOK, 2 * W), BF16),
            jax.ShapeDtypeStruct((1, TOK, W), F32),
        ),
        in_specs=[anywhere] * 6,
        out_specs=(anywhere,) * 5,
        scratch_shapes=scratch,
        compiler_params=pltpu.CompilerParams(
            collective_id=0, has_side_effects=True, vmem_limit_bytes=48 * 1024 * 1024
        ),
        cost_estimate=pl.CostEstimate(flops=1_700_000_000, bytes_accessed=6_000_000, transcendentals=200_000),
    )(acts, gain, kv_grad, master, moment_one, moment_two)


def solution(mesh):
    placed = (
        P("section", "dp", None),
        P("section", None),
        P("section", "dp", None),
        P("section", "dp", None),
        P("section", "dp", None),
        P("section", "dp", None),
    )
    return jax.shard_map(
        per_device,
        mesh=mesh,
        in_specs=placed,
        out_specs=(
            P("section", "dp", None),
            P("section", "dp", None),
            P("section", "dp", None),
            P("dp", "section"),
            P("section", "dp", None),
        ),
        check_vma=False,
    )
```

time: 300 us -> 101 us (0.34)
  waiting for transfers between devices: 203 us -> 0 us
  Pallas kernels: 0 us -> 90.7 us
  blocking collectives: 60.8 us -> 0 us
  between operations: 13.8 us -> 0.66 us
  matrix products: 12.5 us -> 0 us
  local copies, waits for them, and re-layouts: 1.07 us -> 9.45 us
  other arithmetic: 8.26 us -> 0 us
    reduce_scatter x1 -> x0, waiting for transfers between devices: 127 us -> none  [per_device(): lax.psum_scatter(lax.dot_general(hidden, upstream, (((0,), (0,)), ((), ()...]
    pallas_call x0 -> x1, Pallas kernels: none -> 90.7 us  [per_device(): pl.pallas_call(kernel, out_shape=(rows, rows, rows, jax.ShapeDtypeStruct(...]
    all_gather x2 -> x0, waiting for transfers between devices: 76.3 us -> none  [the longest x1 71.3 us: per_device(): lax.all_gather(owned_rows.astype(jnp.bfloat16), 'dp', axis=0, tiled=True)]
    all_to_all x1 -> x0, blocking collectives: 60.8 us -> none  [per_device(): lax.all_to_all(column_blocks, 'section', split_axis=1, concat_axis=1, til...]
    dot_general x3 -> x0, matrix products: 12.5 us -> none  [the longest x1 4.99 us: per_device(): lax.dot_general(hidden, upstream, (((0,), (0,)), ((), ())), preferred_ele...]
    unnamed x12 -> x17, local copies, waits for them, and re-layouts: 0.88 us -> 9.45 us
    reduce_sum x2 -> x0, other arithmetic: 4.66 us -> none  [the longest x1 2.58 us: per_device(): jnp.sum(received, axis=1, dtype=jnp.float32).astype(jnp.bfloat16)]
    convert_element_type x3 -> x0, other arithmetic: 3.59 us -> none  [the longest x1 2.02 us: per_device(): fresh_part = updated.astype(jnp.bfloat16)]
  transfers between devices with their start and end apart: 3 -> 0, of which waited for: 3 -> 0; matrix products, arithmetic and copies ran while one was open for 3% -> 0% of each run, Pallas kernels for 0% -> 0%
where the time goes in v1:
time: 101 us
  Pallas kernels  90.7 us (90%)
  local copies, waits for them, and re-layouts  9.45 us (9%)
    pallas_call x1, Pallas kernels, per_device(): pl.pallas_call(kernel, out_shape=(rows, rows, rows, jax.ShapeDtypeStruct(...  90.7 us
    unnamed x17, local copies, waits for them, and re-layouts  9.45 us

profile of v1, /device:TPU:1, one launch (start us, length us, event | category | flops | bytes accessed | tf_op | source)
XLA Modules:
  0.0 100.8 jit_solution(8533933017285881203)
XLA Ops:
  0.6 0.0 copy-start
  0.6 1.6 %copy-done = bf16[1,128,8192]{2,1,0:T(8,128)(2,1)S(1)} copy-done((bf16[1,128,8192]{2,1,0:T(8,128)(2,1)S(1)}, bf16[1,128,8192]{2,1,0:T(8,128)(2,1)}, u32[]{:S(2)}) %copy-start) | copy-done | bytes 2097176
  2.2 0.0 copy-start.1
  2.2 0.9 copy-done.1
  3.2 0.0 copy-start.2
  3.2 0.9 copy-done.2
  4.1 0.0 copy-start.3
  4.1 0.9 copy-done.3
  5.1 0.0 copy-start.4
  5.1 0.8 copy-done.4
  5.9 0.0 copy-start.5
  5.9 0.8 copy-done.5
  6.7 90.7 %shard_map.101 = (f32[1,256,256]{2,1,0:T(8,128)S(1)}, f32[1,256,256]{2,1,0:T(8,128)S(1)}, f32[1,256,256]{2,1,0:T(8,128)S(1)}, bf16[128,512]{1,0:T(8,128)(2,1)S(1)}, f32[1,128,256]{2,1,0:T(8,128)S(1)}) custom-call(bf16[1,128,8192]{2,1,0:T(8,128)(2,1)S(1)} %copy-done, f32[1,8192]{1,0:T(1,128)S(1)} %copy-done.5, bf16[1,128,256]{2,1,0:T(8,128)(2,1)S(1)} %copy-done.4, ...), custom_call_target="tpu_custom_call" | custom-call | flops 1700000000 | bytes 6000000 | tf_op jit(solution)/shard_map/pallas_call | solution.py:469
  97.4 0.7 copy.16
  98.1 0.7 copy.17
  98.8 0.7 copy.18
  99.5 0.7 copy.19
  100.2 0.7 copy.20
Async XLA Ops:
  0.6 1.6 %copy-start = (bf16[1,128,8192]{2,1,0:T(8,128)(2,1)S(1)}, bf16[1,128,8192]{2,1,0:T(8,128)(2,1)}, u32[]{:S(2)}) copy-start(bf16[1,128,8192]{2,1,0:T(8,128)(2,1)} %acts.1) | copy-start | bytes 6291460
  2.2 0.9 copy-start.1
  3.2 0.9 copy-start.2
  4.1 0.9 copy-start.3
  5.1 0.8 copy-start.4
  5.9 0.8 copy-start.5

commit v2 on v1

v2 whole, which is shorter than its diff:
```python
import contextlib

import jax
import jax.numpy as jnp
from jax import lax
from jax.experimental import pallas as pl
from jax.experimental.pallas import tpu as pltpu
from jax.sharding import PartitionSpec as P

STEP = 20
NORM_EPS = 1e-05
ADAM_EPS = 1e-08
BETA_ONE = 0.9
BETA_TWO = 0.95
LEARN_RATE = 0.00015
DECAY_RATE = 0.1

F32 = jnp.float32
BF16 = jnp.bfloat16
N = 8
D = 8192
TOK = 128
HALF = 64
VMEM_BYTES = 64 * 1024 * 1024
W = 256
SETS = (
    (0, 4), (1, 4), (0, 3), (1, 3), (0, 5), (1, 5), (0, 2), (0, 6),
    (0, 1), (0, 7), (0, 0), (1, 2), (1, 6), (1, 1), (1, 7), (1, 0),
)


def part_of(name):
    return contextlib.nullcontext()


def rows_of(half):
    return pl.ds(half * HALF, HALF)


def wide(a):
    return jnp.concatenate([a, a], axis=-1)


def kernel(
    acts, gain, kv, master, mom1, mom2,
    o_master, o_m1, o_m2, o_in, o_kv,
    a_full, gain_v, mas_v, m1_v, m2_v,
    xa, kvb, kvt, rmb, invc, wt, wn, hid, sc, macc, msend, mrecv, mcol,
    gsum, ysend, yrecv, zsend, zrecv, xsend, xrecv, kvn, kvs, knr, kns,
    nm_v, n1_v, n2_v, oin_v, okv_v,
    l_in, l_acts, s_acts, r_acts, s_kv, r_kv, s_rm, r_rm, s_m, r_m,
    s_w, r_w, s_n, r_n, s_y, r_y, s_z, r_z, s_x, r_x, s_k, r_k, l_out,
):
    section = lax.axis_index("section")
    dp = lax.axis_index("dp")
    z = lax.div(section, 2)
    xh = lax.rem(section, 2)
    y = lax.div(dp, 4)
    q = lax.rem(dp, 4)
    xl = lax.div(q, 2)
    c = lax.rem(q, 2)
    mates = (xl * 2 + (1 - c), (1 - xl) * 2 + c, (1 - xl) * 2 + (1 - c))

    def ring(at, off):
        return lax.rem(at + off, N)

    def y_dev(off):
        return (section, ring(y, off) * 4 + q)

    def z_dev(off):
        return (ring(z, off) * 2 + xh, dp)

    def mate_dev(mate):
        return (section, y * 4 + mate)

    def remote(src, dst, send, recv, device):
        return pltpu.make_async_remote_copy(
            src_ref=src, dst_ref=dst, send_sem=send, recv_sem=recv,
            device_id=device, device_id_type=pl.DeviceIdType.MESH,
        )

    def wait_bytes(ref, sem):
        pltpu.make_async_copy(ref, ref, sem).wait()

    def columns(block):
        return pl.ds(pl.multiple_of(block * 1024 + q * W, W), W)

    loads = [
        pltpu.make_async_copy(master.at[0], mas_v, l_in.at[0]),
        pltpu.make_async_copy(acts.at[0], a_full, l_in.at[1]),
        pltpu.make_async_copy(kv.at[0], kvb.at[q], l_in.at[2]),
        pltpu.make_async_copy(gain, gain_v, l_in.at[3]),
        pltpu.make_async_copy(mom1.at[0], m1_v, l_in.at[4]),
        pltpu.make_async_copy(mom2.at[0], m2_v, l_in.at[5]),
    ]
    for load in loads:
        load.start()

    def own_acts(off):
        block = ring(y, off)
        return pltpu.make_async_copy(acts.at[0, :, columns(block)], xa.at[block, q], l_acts.at[off])

    for off in range(N):
        own_acts(off).start()

    barrier = pltpu.get_barrier_semaphore()
    for fh in range(2):
        for fl in range(2):
            for fc in range(2):
                if fh + fl + fc == 0:
                    continue
                other_h = 1 - xh if fh else xh
                other_l = 1 - xl if fl else xl
                other_c = 1 - c if fc else c
                pl.semaphore_signal(
                    barrier, inc=1, device_id=(z * 2 + other_h, y * 4 + other_l * 2 + other_c),
                    device_id_type=pl.DeviceIdType.MESH,
                )
    for device in (y_dev(1), y_dev(7), z_dev(1), z_dev(7)):
        pl.semaphore_signal(barrier, inc=1, device_id=device, device_id_type=pl.DeviceIdType.MESH)

    with part_of("barrier"):
        pl.semaphore_wait(barrier, 11)

    def send_acts(k):
        half, off = SETS[k]
        block = ring(y, off)
        for mate in mates:
            source = acts.at[0, rows_of(half), pl.ds(pl.multiple_of(block * 1024 + mate * W, W), W)]
            remote(source, xa.at[block, q, rows_of(half)], s_acts.at[k], r_acts.at[k], mate_dev(mate)).start()

    def wait_acts(k):
        half, off = SETS[k]
        if half == 0:
            own_acts(off).wait()
        wait_bytes(xa.at[0, pl.ds(0, 3), rows_of(0)], r_acts.at[k])

    def gather_copy(buffer, send, recv, way, hop, part):
        off = N - hop if way == 0 else hop
        block = buffer.at[ring(y, off), pl.ds(part * 128, 128)]
        return remote(block, block, send.at[way, hop, part], recv.at[way, hop, part], y_dev(1 if way == 0 else 7))

    def gather_hop(buffer, send, recv, hop):
        for k in range(2):
            for way in range(2):
                part = k if way == 0 else 1 - k
                if hop > 0 and (hop < 4 or k == 0):
                    gather_copy(buffer, send, recv, way, hop - 1, part).wait_recv()
                if hop < 3 or (hop == 3 and k == 0):
                    gather_copy(buffer, send, recv, way, hop, part).start()

    def kv_copy(which):
        slot, device = ((q, mates[0]), (q, mates[1]), (mates[1], mates[0]))[which]
        return remote(kvb.at[slot], kvb.at[slot], s_kv.at[which], r_kv.at[which], mate_dev(device))

    loads[2].wait()
    kv_copy(1).start()
    kv_copy(0).start()
    send_acts(0)
    send_acts(1)
    with part_of("wt"):
        loads[0].wait()
        wt[y] = jnp.transpose(mas_v[...]).astype(BF16)
    gather_hop(wt, s_w, r_w, 0)

    with part_of("squares"):
        loads[1].wait()

        def add_squares(step, total):
            part = a_full[:, pl.ds(pl.multiple_of(step * 512, 512), 512)].astype(F32)
            part = part * part
            return total + ((part[:, :128] + part[:, 128:256]) + (part[:, 256:384] + part[:, 384:]))

        squares = lax.fori_loop(0, 16, add_squares, jnp.zeros((TOK, 128), F32))
        mean_row = jnp.sum(jnp.transpose(squares), axis=0, keepdims=True) / D
        rmb[q] = jnp.broadcast_to(jnp.sqrt(mean_row + NORM_EPS), (8, 128))
    for mate in mates:
        remote(rmb.at[q], rmb.at[q], s_rm, r_rm, mate_dev(mate)).start()
    for k in range(2, 11):
        send_acts(k)
    macc[...] = jnp.zeros_like(macc)
    loads[3].wait()

    with part_of("kv_wait"):
        kv_copy(1).wait_recv()
        kv_copy(2).start()
    with part_of("old_hop1"):
        gather_hop(wt, s_w, r_w, 1)
    with part_of("kv_wait"):
        kv_copy(0).wait_recv()
        kv_copy(2).wait_recv()
    with part_of("rm_wait"):
        wait_bytes(rmb.at[pl.ds(0, 3)], r_rm)

    def prepare(slot, carry):
        root = jnp.transpose(jnp.broadcast_to(rmb[slot][0:1, :], (128, 128)))
        invc[slot] = 1.0 / root
        kvt[slot] = jnp.transpose(kvb[slot].astype(F32)).astype(BF16)
        return carry

    with part_of("prepare"):
        lax.fori_loop(0, 4, prepare, 0)

    def hide(half, block):
        gain_row = gain_v[:, columns(block)]

        def one(slot, carry):
            unit = xa[block, slot, rows_of(half), :].astype(F32) * wide(invc[slot, rows_of(half), :])
            hid[block, slot, rows_of(half), :] = (unit * gain_row).astype(BF16)
            return carry

        lax.fori_loop(0, 4, one, 0)

    def back(half, block):
        gain_row = gain_v[:, columns(block)]
        product = jnp.dot(
            kvb[:, rows_of(half), :].reshape(4 * HALF, W), wt[block], preferred_element_type=F32
        )
        sc[block, :, rows_of(half), :] = product.reshape(4, HALF, W)

        def one(slot, carry):
            unit = xa[block, slot, rows_of(half), :].astype(F32) * wide(invc[slot, rows_of(half), :])
            scaled = sc[block, slot, rows_of(half), :] * gain_row
            sc[block, slot, rows_of(half), :] = scaled
            both = scaled * unit
            macc[half, slot] += both[:, :128] + both[:, 128:]
            return carry

        lax.fori_loop(0, 4, one, 0)

    def send_means(half):
        msend[half] = jnp.zeros((8, 128), F32)
        for pair in range(2):
            both = macc[half, pl.ds(pair * 2, 2)].reshape(128, 128)
            msend[half, pair : pair + 1, :] = jnp.sum(jnp.transpose(both), axis=0, keepdims=True)
        for r, mate in enumerate(mates):
            remote(msend.at[half], mrecv.at[half, r], s_m.at[half, r], r_m.at[half, r], mate_dev(mate)).start()

    def get_means(half):
        for r, mate in enumerate(mates):
            remote(msend.at[half], mrecv.at[half, r], s_m.at[half, r], r_m.at[half, r], mate_dev(mate)).wait_recv()
        total = ((msend[half] + mrecv[half, 0]) + (mrecv[half, 1] + mrecv[half, 2])) / D
        for pair in range(2):
            column = jnp.transpose(jnp.broadcast_to(total[pair : pair + 1, :], (128, 128)))
            mcol[half, pl.ds(pair * 2, 2)] = column.reshape(2, HALF, 128)

    def branch(half, block, slot):
        inv = wide(invc[slot, rows_of(half), :])
        unit = xa[block, slot, rows_of(half), :].astype(F32) * inv
        return ((sc[block, slot, rows_of(half), :] - unit * wide(mcol[half, slot])) * inv).astype(BF16)

    def z_copy(half, way, step, part):
        slots = pl.ds(2 * part, 2)
        return remote(
            zsend.at[half, way, step, slots], zrecv.at[half, way, step, slots],
            s_z.at[half, way, step, part], r_z.at[half, way, step, part], z_dev(1 if way == 0 else 7),
        )

    def z_step(half, step):
        for k in range(2):
            for way in range(2):
                part = 1 - way if k == 0 else way
                if step == 0 and k == 0:
                    continue
                block = ring(z, 4 - step if way == 0 else 4 + step)
                adds = step > 1 or (step == 1 and part == way)
                if adds:
                    z_copy(half, way, step - 1, part).wait_recv()
                for slot in (2 * part, 2 * part + 1):
                    own = branch(half, block, slot)
                    if adds:
                        own = (own.astype(F32) + zrecv[half, way, step - 1, slot].astype(F32)).astype(BF16)
                    zsend[half, way, step, slot] = own
                z_copy(half, way, step, part).start()

    x_section = z * 2 + xl
    x_source = xh * 2 + c

    def x_copy(half, slot):
        return remote(
            xsend.at[half, slot], xrecv.at[half, x_source], s_x.at[half, slot], r_x.at[half, x_source],
            (x_section, y * 4 + slot),
        )

    def stays(slot):
        return jnp.logical_and(xh == xl, q == slot)

    def z_last(half):
        for way in range(2):
            for part in range(2):
                z_copy(half, way, 3, part).wait_recv()

        def one(slot, carry):
            total = branch(half, z, slot).astype(F32)
            total = total + (zrecv[half, 0, 3, slot].astype(F32) + zrecv[half, 1, 3, slot].astype(F32))
            xsend[half, slot] = total.astype(BF16)
            return carry

        lax.fori_loop(0, 4, one, 0)
        for slot in range(4):
            @pl.when(stays(slot))
            def _():
                pltpu.make_async_copy(xsend.at[half, slot], xrecv.at[half, x_source], r_x.at[half, x_source]).start()

            @pl.when(jnp.logical_not(stays(slot)))
            def _():
                x_copy(half, slot).start()

    def x_last(half):
        for source in range(4):
            wait_bytes(xrecv.at[half, source], r_x.at[half, source])
        for col in range(2):
            total = xrecv[half, col].astype(F32) + xrecv[half, 2 + col].astype(F32)
            oin_v[rows_of(half), col * W : (col + 1) * W] = total.astype(BF16)

    def old_hop(hop):
        with part_of("old_hop%d" % hop):
            gather_hop(wt, s_w, r_w, hop)

    def new_hop(hop):
        with part_of("new_hop%d" % hop):
            gather_hop(wn, s_n, r_n, hop)

    def arrive(k):
        with part_of("acts_wait%d" % k):
            wait_acts(k)
        with part_of("hide"):
            half, off = SETS[k]
            hide(half, ring(y, off))

    def backs(*pairs):
        with part_of("back"):
            for half, off in pairs:
                back(half, ring(y, off))

    def grad(off):
        with part_of("grad"):
            block = ring(y, off)
            total = None
            for slot in range(4):
                product = jnp.dot(kvt[slot], hid[block, slot], preferred_element_type=F32).astype(BF16).astype(F32)
                total = product if total is None else total + product
            gsum[block] = total

    def means(half):
        with part_of("means%d" % half):
            get_means(half)

    def z_part(half, step):
        with part_of("z%d_%d" % (half, step)):
            if step < 4:
                z_step(half, step)
            else:
                z_last(half)

    def x_part(half):
        with part_of("x%d" % half):
            x_last(half)

    def y_copy(way, step, part):
        rows = pl.ds(part * 128, 128)
        return remote(
            ysend.at[way, step, rows], yrecv.at[way, step, rows], s_y.at[way, step, part], r_y.at[way, step, part],
            y_dev(1 if way == 0 else 7),
        )

    def y_step(step):
        for k in range(2):
            for way in range(2):
                part = 1 - way if k == 0 else way
                if step == 0 and k == 0:
                    continue
                block = ring(y, 4 - step if way == 0 else 4 + step)
                rows = pl.ds(part * 128, 128)
                total = gsum[block, rows]
                if step > 1 or (step == 1 and part == way):
                    y_copy(way, step - 1, part).wait_recv()
                    total = total + yrecv[way, step - 1, rows].astype(F32)
                ysend[way, step, rows] = total.astype(BF16)
                y_copy(way, step, part).start()

    def y_part(step):
        with part_of("y%d" % step):
            if step < 4:
                y_step(step)
                return
            for part in range(2):
                for way in range(2):
                    y_copy(way, 3, part).wait_recv()

    def next_part(off):
        with part_of("next"):
            block = ring(y, off)
            part = jnp.dot(hid[block].reshape(4 * TOK, W), wn[block], preferred_element_type=F32).reshape(4, TOK, W)
            kvn[...] = part if off == 0 else kvn[...] + part

    arrive(0)
    arrive(1)
    grad(4)
    arrive(2)
    arrive(3)
    old_hop(2)
    y_part(0)
    arrive(4)
    arrive(5)
    grad(3)
    grad(5)
    old_hop(3)
    y_part(1)
    send_acts(11)
    send_acts(12)
    backs((0, 3), (1, 3), (0, 5), (1, 5))
    arrive(6)
    backs((0, 2))
    arrive(7)
    backs((0, 6))
    arrive(8)
    backs((0, 1))
    old_hop(4)
    backs((0, 4), (1, 4))
    arrive(9)
    backs((0, 7))
    arrive(10)
    backs((0, 0))
    send_means(0)
    for k in range(13, 16):
        send_acts(k)
    arrive(11)
    backs((1, 2))
    grad(2)
    arrive(12)
    backs((1, 6))
    grad(6)
    y_part(2)
    means(0)
    z_part(0, 0)
    arrive(13)
    backs((1, 1))
    grad(1)
    arrive(14)
    backs((1, 7))
    grad(7)
    arrive(15)
    backs((1, 0))
    send_means(1)
    y_part(3)
    grad(0)
    z_part(0, 1)
    means(1)
    z_part(1, 0)
    y_part(4)

    with part_of("adam"):
        for load in loads[4:6]:
            load.wait()
        gradient = jnp.transpose(gsum[y] + (yrecv[0, 3].astype(F32) + yrecv[1, 3].astype(F32)))
        old = mas_v[...]
        first_new = BETA_ONE * m1_v[...] + (1.0 - BETA_ONE) * gradient
        second_new = BETA_TWO * m2_v[...] + (1.0 - BETA_TWO) * gradient * gradient
        direction = (
            first_new / (1.0 - BETA_ONE**STEP) / (jnp.sqrt(second_new / (1.0 - BETA_TWO**STEP)) + ADAM_EPS)
        )
        updated = old - LEARN_RATE * (direction + DECAY_RATE * old)
        wn[y] = updated.astype(BF16)
        new_hop(0)
        nm_v[...] = updated
        n1_v[...] = first_new
        n2_v[...] = second_new
    stores = [
        pltpu.make_async_copy(nm_v, o_master.at[0], l_out.at[0]),
        pltpu.make_async_copy(n1_v, o_m1.at[0], l_out.at[1]),
        pltpu.make_async_copy(n2_v, o_m2.at[0], l_out.at[2]),
    ]
    for store in stores:
        store.start()

    next_part(0)
    z_part(0, 2)
    z_part(1, 1)
    new_hop(1)
    next_part(1)
    next_part(7)
    z_part(0, 3)
    z_part(1, 2)
    new_hop(2)
    next_part(2)
    next_part(6)
    z_part(0, 4)
    z_part(1, 3)
    new_hop(3)
    next_part(3)
    next_part(5)
    x_part(0)
    z_part(1, 4)
    new_hop(4)
    next_part(4)

    def next_copy(r):
        if r == 0:
            return remote(kvn.at[mates[0]], knr, s_k.at[0], r_k.at[0], mate_dev(mates[0]))
        return remote(kvs.at[r - 1], kns.at[r - 1], s_k.at[r], r_k.at[r], mate_dev(mates[r]))

    for r in (1, 2):
        kvs[r - 1] = kvn[mates[r]].astype(BF16)
        next_copy(r).start()
    next_copy(0).start()
    x_part(1)
    stores.append(pltpu.make_async_copy(oin_v, o_in, l_out.at[4]))
    stores[-1].start()
    with part_of("next_wait"):
        for r in range(3):
            next_copy(r).wait_recv()
    okv_v[...] = (kvn[q] + knr[...]) + (kns[0].astype(F32) + kns[1].astype(F32))
    stores.append(pltpu.make_async_copy(okv_v, o_kv.at[0], l_out.at[3]))
    stores[-1].start()

    wait_bytes(rmb.at[pl.ds(0, 3)], s_rm)
    for which in range(3):
        kv_copy(which).wait_send()
        next_copy(which).wait_send()
    for k in range(len(SETS)):
        wait_bytes(xa.at[0, pl.ds(0, 3), rows_of(0)], s_acts.at[k])
    for half in range(2):
        for r, mate in enumerate(mates):
            remote(msend.at[half], mrecv.at[half, r], s_m.at[half, r], r_m.at[half, r], mate_dev(mate)).wait_send()
        for slot in range(4):
            @pl.when(jnp.logical_not(stays(slot)))
            def _():
                x_copy(half, slot).wait_send()
    for way in range(2):
        for step in range(4):
            for part in range(2):
                if step < 3 or part == way:
                    gather_copy(wt, s_w, r_w, way, step, part).wait_send()
                    gather_copy(wn, s_n, r_n, way, step, part).wait_send()
                if step > 0 or part == way:
                    y_copy(way, step, part).wait_send()
                    z_copy(0, way, step, part).wait_send()
                    z_copy(1, way, step, part).wait_send()
    for store in stores:
        store.wait()


def write_out(*refs):
    sources, targets, held, got, done = refs[:5], refs[5:10], refs[10:15], refs[15], refs[16]
    loads = [pltpu.make_async_copy(sources[i], held[i], got.at[i]) for i in range(5)]
    stores = [pltpu.make_async_copy(held[i], targets[i], done.at[i]) for i in range(5)]
    for load in loads:
        load.start()
    for load, store in zip(loads, stores):
        load.wait()
        store.start()
    for store in stores:
        store.wait()


def per_device(acts, gain, kv_grad, master, moment_one, moment_two):
    anywhere = pl.BlockSpec(memory_space=pl.ANY)
    vmem = pltpu.VMEM
    dma = pltpu.SemaphoreType.DMA
    rows = jax.ShapeDtypeStruct((1, W, W), F32)
    scratch = [
        vmem((TOK, D), BF16),
        vmem((1, D), F32),
        vmem((W, W), F32), vmem((W, W), F32), vmem((W, W), F32),
        vmem((N, 4, TOK, W), BF16),
        vmem((4, TOK, W), BF16),
        vmem((4, W, TOK), BF16),
        vmem((4, 8, 128), F32),
        vmem((4, TOK, 128), F32),
        vmem((N, W, W), BF16),
        vmem((N, W, W), BF16),
        vmem((N, 4, TOK, W), BF16),
        vmem((N, 4, TOK, W), F32),
        vmem((2, 4, HALF, 128), F32),
        vmem((2, 8, 128), F32),
        vmem((2, 3, 8, 128), F32),
        vmem((2, 4, HALF, 128), F32),
        vmem((N, W, W), F32),
        vmem((2, 4, W, W), BF16), vmem((2, 4, W, W), BF16),
        vmem((2, 2, 4, 4, HALF, W), BF16), vmem((2, 2, 4, 4, HALF, W), BF16),
        vmem((2, 4, HALF, W), BF16), vmem((2, 4, HALF, W), BF16),
        vmem((4, TOK, W), F32), vmem((2, TOK, W), BF16),
        vmem((TOK, W), F32), vmem((2, TOK, W), BF16),
        vmem((W, W), F32), vmem((W, W), F32), vmem((W, W), F32),
        vmem((TOK, 2 * W), BF16),
        vmem((TOK, W), F32),
        dma((6,)), dma((N,)), dma((2 * N,)), dma((2 * N,)),
        dma((3,)), dma((3,)), dma, dma,
        dma((2, 3)), dma((2, 3)),
        dma((2, 4, 2)), dma((2, 4, 2)), dma((2, 4, 2)), dma((2, 4, 2)),
        dma((2, 4, 2)), dma((2, 4, 2)),
        dma((2, 2, 4, 2)), dma((2, 2, 4, 2)),
        dma((2, 4)), dma((2, 4)),
        dma((3,)), dma((3,)), dma((5,)),
    ]
    shapes = (
        rows, rows, rows,
        jax.ShapeDtypeStruct((TOK, 2 * W), BF16),
        jax.ShapeDtypeStruct((1, TOK, W), F32),
    )
    results = pl.pallas_call(
        kernel,
        out_shape=shapes,
        in_specs=[anywhere] * 6,
        out_specs=(anywhere,) * 5,
        scratch_shapes=scratch,
        compiler_params=pltpu.CompilerParams(
            collective_id=0, has_side_effects=True, vmem_limit_bytes=VMEM_BYTES
        ),
        cost_estimate=pl.CostEstimate(flops=1_700_000_000, bytes_accessed=6_000_000, transcendentals=200_000),
    )(acts, gain, kv_grad, master, moment_one, moment_two)
    return pl.pallas_call(
        write_out,
        out_shape=shapes,
        in_specs=[anywhere] * 5,
        out_specs=(anywhere,) * 5,
        scratch_shapes=[vmem(shape.shape, shape.dtype) for shape in shapes] + [dma((5,)), dma((5,))],
        compiler_params=pltpu.CompilerParams(vmem_limit_bytes=VMEM_BYTES),
        cost_estimate=pl.CostEstimate(flops=0, bytes_accessed=2_100_000, transcendentals=0),
    )(*results)


def solution(mesh):
    placed = (
        P("section", "dp", None),
        P("section", None),
        P("section", "dp", None),
        P("section", "dp", None),
        P("section", "dp", None),
        P("section", "dp", None),
    )
    return jax.shard_map(
        per_device,
        mesh=mesh,
        in_specs=placed,
        out_specs=(
            P("section", "dp", None),
            P("section", "dp", None),
            P("section", "dp", None),
            P("dp", "section"),
            P("section", "dp", None),
        ),
        check_vma=False,
    )
```

time: 101 us -> 74.7 us (0.74)
  Pallas kernels: 90.7 us -> 73.9 us
  local copies, waits for them, and re-layouts: 9.45 us -> 0 us
    pallas_call x1 -> x2, Pallas kernels: 90.7 us -> 73.9 us  [the longest x1 71.9 us: per_device(): pl.pallas_call(kernel, out_shape=shapes, in_specs=[anywhere] * 6, out_spe...]
    unnamed x17 -> x0, local copies, waits for them, and re-layouts: 9.45 us -> none
where the time goes in v2:
time: 74.7 us; the launch traced here: 74.6 us
  Pallas kernels  73.9 us (99%)
    pallas_call x1, Pallas kernels, per_device(): pl.pallas_call(kernel, out_shape=shapes, in_specs=[anywhere] * 6, out_spe...  71.9 us
    pallas_call x1, Pallas kernels, per_device(): pl.pallas_call(write_out, out_shape=shapes, in_specs=[anywhere] * 5, out_...  1.99 us

profile of v2, /device:TPU:1, one launch (start us, length us, event | category | flops | bytes accessed | tf_op | source)
XLA Modules:
  0.0 74.6 jit_solution(675568640461651645)
XLA Ops:
  0.6 71.9 %shard_map.101 = (f32[1,256,256]{2,1,0:T(8,128)}, f32[1,256,256]{2,1,0:T(8,128)}, f32[1,256,256]{2,1,0:T(8,128)}, bf16[128,512]{1,0:T(8,128)(2,1)}, f32[1,128,256]{2,1,0:T(8,128)}) custom-call(bf16[1,128,8192]{2,1,0:T(8,128)(2,1)} %acts.1, f32[1,8192]{1,0:T(1,128)} %gain.1, bf16[1,128,256]{2,1,0:T(8,128)(2,1)} %kv.1, f32[1,256,256]{2,1,0:T(8,128)} %master.1, ...), custom_call_target="tpu_custom_call" | custom-call | flops 1700000000 | bytes 6000000 | tf_op jit(solution)/shard_map/pallas_call | solution.py:602
  72.6 2.0 %shard_map.102 = (f32[1,256,256]{2,1,0:T(8,128)}, f32[1,256,256]{2,1,0:T(8,128)}, f32[1,256,256]{2,1,0:T(8,128)}, bf16[128,512]{1,0:T(8,128)(2,1)}, f32[1,128,256]{2,1,0:T(8,128)}) custom-call(f32[1,256,256]{2,1,0:T(8,128)} %get-tuple-element.10.refs_0_, f32[1,256,256]{2,1,0:T(8,128)} %get-tuple-element.11.refs_1_, ...), custom_call_target="tpu_custom_call" | custom-call | bytes 2100000 | tf_op jit(solution)/shard_map/pallas_call | solution.py:613

commit v3 on v0

v3 whole, which is shorter than its diff:
```python
import contextlib

import jax
import jax.numpy as jnp
from jax import lax
from jax.experimental import pallas as pl
from jax.experimental.pallas import tpu as pltpu
from jax.sharding import PartitionSpec as P

STEP = 20
NORM_EPS = 1e-05
ADAM_EPS = 1e-08
BETA_ONE = 0.9
BETA_TWO = 0.95
LEARN_RATE = 0.00015
DECAY_RATE = 0.1

F32 = jnp.float32
BF16 = jnp.bfloat16
MESH = pl.DeviceIdType.MESH
N = 8
D = 8192
TOK = 128
W = 256
VMEM_BYTES = 48 * 1024 * 1024
GROUPS = ((0, 64), (64, 32), (96, 32))
SETS = (
    (0, 0), (0, 7), (0, 1), (0, 2), (0, 6), (0, 5), (0, 3), (0, 4),
    (1, 4), (2, 4), (1, 3), (2, 3), (1, 5), (2, 5), (1, 2), (1, 6),
    (2, 6), (2, 2), (1, 7), (2, 7), (1, 1), (2, 1), (1, 0), (2, 0),
)
AHEAD = 5
HOLD = 24
STEPS = (
    ("relay",), ("old", 1, 0), ("old", 1, 1), ("prepare",), ("arrive", 0), ("arrive", 1), ("back", 0, 0),
    ("back", 0, 7), ("old", 2, 0), ("arrive", 2), ("back", 0, 1), ("old", 2, 1), ("arrive", 3), ("back", 0, 2),
    ("arrive", 4), ("back", 0, 6), ("old", 3, 0), ("arrive", 5), ("old", 3, 1), ("back", 0, 5), ("arrive", 6),
    ("back", 0, 3), ("old", 4, 0), ("arrive", 7), ("back", 0, 4), ("put", 0), ("arrive", 8), ("back", 1, 4),
    ("arrive", 9), ("grad", 4), ("ysum", 0, 0, 1), ("ysum", 1, 0, 1), ("back", 2, 4), ("arrive", 10), ("back", 1, 3),
    ("arrive", 11), ("grad", 3), ("back", 2, 3), ("arrive", 12), ("get", 0), ("zsum", 0, 0, 1, 0),
    ("zsum", 0, 1, 0, 0), ("zsum", 0, 0, 1, 1), ("zsum", 0, 1, 0, 1), ("back", 1, 5), ("arrive", 13), ("grad", 5),
    ("ysum", 0, 1, 0), ("ysum", 0, 1, 1), ("ysum", 1, 1, 0), ("back", 2, 5), ("arrive", 14), ("back", 1, 2),
    ("ysum", 1, 1, 1), ("arrive", 15), ("back", 1, 6), ("arrive", 16), ("grad", 6), ("zsum", 0, 1, 1, 0),
    ("back", 2, 6), ("arrive", 17), ("grad", 2), ("zsum", 0, 2, 0, 0), ("ysum", 0, 2, 0), ("back", 2, 2),
    ("arrive", 18), ("back", 1, 7), ("zsum", 0, 1, 1, 1), ("ysum", 0, 2, 1), ("arrive", 19), ("grad", 7),
    ("zsum", 0, 2, 0, 1), ("ysum", 1, 2, 0), ("back", 2, 7), ("arrive", 20), ("back", 1, 1), ("zsum", 0, 2, 1, 0),
    ("ysum", 1, 2, 1), ("arrive", 21), ("grad", 1), ("zsum", 0, 3, 0, 0), ("ysum", 0, 3, 0), ("back", 2, 1),
    ("arrive", 22), ("back", 1, 0), ("put", 1), ("zsum", 0, 2, 1, 1), ("ysum", 0, 3, 1), ("arrive", 23), ("grad", 0),
    ("back", 2, 0), ("put", 2), ("zsum", 0, 3, 0, 1), ("ysum", 1, 3, 0), ("zsum", 0, 3, 1, 0), ("ysum", 1, 3, 1),
    ("get", 1), ("zsum", 1, 0, 1, 0), ("zsum", 1, 1, 0, 0), ("get", 2), ("adam", 0), ("zsum", 2, 0, 1, 0),
    ("zsum", 2, 1, 0, 0), ("zsum", 0, 3, 1, 1), ("next", 0, 0), ("adam", 1), ("next", 1, 0), ("zsum", 1, 1, 1, 0),
    ("zsum", 1, 2, 0, 0), ("new", 0, 1, 0), ("zsum", 2, 1, 1, 0), ("new", 0, 1, 1), ("next", 0, 1), ("next", 0, 7),
    ("zsum", 2, 2, 0, 0), ("new", 1, 1, 0), ("zlast", 0), ("new", 1, 1, 1), ("next", 1, 1), ("next", 1, 7),
    ("zsum", 1, 2, 1, 0), ("new", 0, 2, 0), ("zsum", 1, 3, 0, 0), ("new", 0, 2, 1), ("next", 0, 2), ("next", 0, 6),
    ("zsum", 2, 2, 1, 0), ("new", 1, 2, 0), ("zsum", 2, 3, 0, 0), ("new", 1, 2, 1), ("next", 1, 2), ("next", 1, 6),
    ("zsum", 1, 3, 1, 0), ("new", 0, 3, 0), ("new", 0, 3, 1), ("next", 0, 3), ("next", 0, 5), ("zsum", 2, 3, 1, 0),
    ("new", 1, 3, 0), ("xlast", 0), ("new", 1, 3, 1), ("next", 1, 3), ("next", 1, 5), ("zlast", 1), ("new", 0, 4, 0),
    ("next", 0, 4), ("share", 0), ("zlast", 2), ("new", 1, 4, 0), ("next", 1, 4), ("share", 1), ("cross", 0),
    ("cross", 1), ("xlast", 1), ("finish", 0), ("xlast", 2), ("finish", 1),
)

def part_of(name):
    return contextlib.nullcontext()


def rows_of(group):
    return pl.ds(*GROUPS[group])


def part_rows(part):
    return pl.ds(part * 128, 128)


def wide(a):
    return jnp.concatenate([a, a], axis=-1)


def kernel(
    acts, gain, kv, master, mom1, mom2,
    o_master, o_m1, o_m2, o_in, o_kv,
    a_full, gain_v, mas_v, m1_v, m2_v,
    xa, kvb, kvt, rmb, invc, wt, wn, hid, sc, macc, msend, mrecv, mcol,
    gsum, ysend, yrecv, zsend, zrecv, xsend, xrecv, kvn, kvs, knc, knr, kns,
    l_in, l_acts, s_acts, s_kv, s_rm, s_m, s_w, s_n, s_y, s_z, s_x, s_k, s_kc,
    r_acts, r_kv, r_rm, r_m, r_w, r_n, r_y, r_z, r_x, r_k, r_kc,
):
    section = lax.axis_index("section")
    dp = lax.axis_index("dp")
    z = lax.div(section, 2)
    xh = lax.rem(section, 2)
    y = lax.div(dp, 4)
    q = lax.rem(dp, 4)
    xl = lax.div(q, 2)
    c = lax.rem(q, 2)
    mates = (xl * 2 + (1 - c), (1 - xl) * 2 + c, (1 - xl) * 2 + (1 - c))

    def ring(at, off):
        return lax.rem(at + off, N)

    def y_dev(off):
        return (section, ring(y, off) * 4 + q)

    def z_dev(off):
        return (ring(z, off) * 2 + xh, dp)

    def mate_dev(mate):
        return (section, y * 4 + mate)

    def remote(src, dst, send, recv, device):
        return pltpu.make_async_remote_copy(
            src_ref=src, dst_ref=dst, send_sem=send, recv_sem=recv, device_id=device, device_id_type=MESH
        )

    def wait_bytes(ref, sem):
        pltpu.make_async_copy(ref, ref, sem).wait()

    def columns(block):
        return pl.ds(pl.multiple_of(block * 1024 + q * W, W), W)

    barrier = pltpu.get_barrier_semaphore()
    for fh in range(2):
        for fl in range(2):
            for fc in range(2):
                if fh + fl + fc == 0:
                    continue
                other_h = 1 - xh if fh else xh
                other_l = 1 - xl if fl else xl
                other_c = 1 - c if fc else c
                device = (z * 2 + other_h, y * 4 + other_l * 2 + other_c)
                pl.semaphore_signal(barrier, inc=1, device_id=device, device_id_type=MESH)
    for device in (y_dev(1), y_dev(7), z_dev(1), z_dev(7)):
        pl.semaphore_signal(barrier, inc=1, device_id=device, device_id_type=MESH)

    loads = [
        pltpu.make_async_copy(kv.at[0], kvb.at[q], l_in.at[0]),
        pltpu.make_async_copy(master.at[0], mas_v, l_in.at[1]),
        pltpu.make_async_copy(acts.at[0], a_full, l_in.at[2]),
        pltpu.make_async_copy(gain, gain_v, l_in.at[3]),
        pltpu.make_async_copy(mom1.at[0], m1_v, l_in.at[4]),
        pltpu.make_async_copy(mom2.at[0], m2_v, l_in.at[5]),
    ]
    for load in loads:
        load.start()
    for off in range(N):
        block = ring(y, off)
        pltpu.make_async_copy(acts.at[0, :, columns(block)], xa.at[block, q], l_acts).start()

    with part_of("barrier"):
        pl.semaphore_wait(barrier, 11)

    def send_acts(k):
        group, off = SETS[k]
        rows = rows_of(group)
        block = ring(y, off)
        for mate in mates:
            source = acts.at[0, rows, pl.ds(pl.multiple_of(block * 1024 + mate * W, W), W)]
            remote(source, xa.at[block, q, rows], s_acts, r_acts.at[k], mate_dev(mate)).start()

    def kv_copy(which):
        slot, mate = ((q, mates[0]), (q, mates[1]), (mates[1], mates[0]))[which]
        return remote(kvb.at[slot], kvb.at[slot], s_kv, r_kv.at[which], mate_dev(mate))

    def gather_send(buffer, send, recv, hop, k):
        for way in range(2):
            block = ring(y, N - hop if way == 0 else hop)
            rows = buffer.at[block, part_rows(k if way == 0 else 1 - k)]
            remote(rows, rows, send, recv.at[hop, k], y_dev(1 if way == 0 else 7)).start()

    def gather_step(buffer, send, recv, hop, k):
        wait_bytes(buffer.at[0], recv.at[hop - 1, k])
        if hop < 3 or (hop == 3 and k == 0):
            gather_send(buffer, send, recv, hop, k)

    loads[0].wait()
    kv_copy(1).start()
    kv_copy(0).start()
    send_acts(0)
    send_acts(1)
    with part_of("wt"):
        loads[1].wait()
        wt[y] = jnp.transpose(mas_v[...]).astype(BF16)
    for k in range(2):
        gather_send(wt, s_w, r_w, 0, k)

    with part_of("squares"):
        loads[2].wait()

        def add_squares(step, total):
            part = a_full[:, pl.ds(pl.multiple_of(step * 512, 512), 512)].astype(F32)
            part = part * part
            return total + ((part[:, :128] + part[:, 128:256]) + (part[:, 256:384] + part[:, 384:]))

        squares = lax.fori_loop(0, 16, add_squares, jnp.zeros((TOK, 128), F32))
        mean_row = jnp.sum(jnp.transpose(squares), axis=0, keepdims=True) / D
        rmb[q] = jnp.broadcast_to(jnp.sqrt(mean_row + NORM_EPS), (8, 128))
    for mate in mates:
        remote(rmb.at[q], rmb.at[q], s_rm, r_rm, mate_dev(mate)).start()
    for k in range(2, min(AHEAD, HOLD)):
        send_acts(k)
    sent = [min(AHEAD, HOLD), False, -1]
    macc[...] = jnp.zeros_like(macc)
    loads[3].wait()
    wait_bytes(xa.at[pl.ds(0, 2)], l_acts)

    def relay():
        kv_copy(1).wait_recv()
        kv_copy(2).start()

    def prepare():
        kv_copy(0).wait_recv()
        kv_copy(2).wait_recv()
        wait_bytes(rmb.at[pl.ds(0, 3)], r_rm)

        def one(slot, carry):
            root = jnp.transpose(jnp.broadcast_to(rmb[slot][0:1, :], (128, 128)))
            invc[slot] = 1.0 / root
            kvt[slot] = jnp.transpose(kvb[slot].astype(F32)).astype(BF16)
            return carry

        lax.fori_loop(0, 4, one, 0)

    def old(hop, k):
        gather_step(wt, s_w, r_w, hop, k)

    def new(half, hop, k):
        gather_step(wn.at[:, half], s_n, r_n.at[half], hop, k)

    def feed(k):
        for later in range(sent[0], min(k + 1 + AHEAD, len(SETS) if sent[1] else HOLD)):
            send_acts(later)
            sent[0] = later + 1
        sent[2] = k

    def arrive(k):
        group, off = SETS[k]
        rows = rows_of(group)
        wait_bytes(xa.at[0, pl.ds(0, 3), rows], r_acts.at[k])
        feed(k)
        block = ring(y, off)
        gain_row = gain_v[:, columns(block)]

        def one(slot, carry):
            unit = xa[block, slot, rows, :].astype(F32) * wide(invc[slot, rows, :])
            hid[block, slot, rows, :] = (unit * gain_row).astype(BF16)
            return carry

        lax.fori_loop(0, 4, one, 0)

    def back(group, off):
        rows = rows_of(group)
        count = GROUPS[group][1]
        block = ring(y, off)
        gain_row = gain_v[:, columns(block)]
        product = jnp.dot(kvb[:, rows, :].reshape(4 * count, W), wt[block], preferred_element_type=F32)
        sc[block, :, rows, :] = product.reshape(4, count, W)

        def one(slot, carry):
            unit = xa[block, slot, rows, :].astype(F32) * wide(invc[slot, rows, :])
            scaled = sc[block, slot, rows, :] * gain_row
            sc[block, slot, rows, :] = scaled
            both = scaled * unit
            macc[slot, rows, :] += both[:, :128] + both[:, 128:]
            return carry

        lax.fori_loop(0, 4, one, 0)

    def grad(off):
        block = ring(y, off)
        total = None
        for slot in range(4):
            product = jnp.dot(kvt[slot], hid[block, slot], preferred_element_type=F32).astype(BF16).astype(F32)
            total = product if total is None else total + product
        gsum[block] = total

    def put(group):
        rows = rows_of(group)
        slots = 128 // GROUPS[group][1]
        msend[group] = jnp.zeros((8, 128), F32)
        for row in range(4 // slots):
            both = macc[pl.ds(row * slots, slots), rows].reshape(128, 128)
            msend[group, row : row + 1, :] = jnp.sum(jnp.transpose(both), axis=0, keepdims=True)
        for r, mate in enumerate(mates):
            remote(msend.at[group], mrecv.at[group, r], s_m, r_m.at[group], mate_dev(mate)).start()
        sent[1] = True
        feed(sent[2])

    def get(group):
        wait_bytes(mrecv.at[group], r_m.at[group])
        total = ((msend[group] + mrecv[group, 0]) + (mrecv[group, 1] + mrecv[group, 2])) / D
        slots = 128 // GROUPS[group][1]
        for row in range(4 // slots):
            column = jnp.transpose(jnp.broadcast_to(total[row : row + 1, :], (128, 128)))
            mcol[pl.ds(row * slots, slots), rows_of(group)] = column.reshape(slots, GROUPS[group][1], 128)

    def branch(group, block, slot):
        rows = rows_of(group)
        inv = wide(invc[slot, rows, :])
        unit = xa[block, slot, rows, :].astype(F32) * inv
        return ((sc[block, slot, rows, :] - unit * wide(mcol[slot, rows])) * inv).astype(BF16)

    def ysum(half, step, k):
        adds = step > 1 or (step == 1 and k == 1)
        if adds:
            wait_bytes(yrecv.at[0, 0, part_rows(0)], r_y.at[half, step - 1, k])
        for way in range(2):
            part = way if k == 1 else 1 - way
            rows = pl.ds(half * 128 + part * 64, 64)
            total = gsum[ring(y, 4 - step if way == 0 else 4 + step), rows]
            if adds:
                total = total + yrecv[way, step - 1, rows].astype(F32)
            ysend[way, step, rows] = total.astype(BF16)
            remote(
                ysend.at[way, step, rows], yrecv.at[way, step, rows], s_y, r_y.at[half, step, k],
                y_dev(1 if way == 0 else 7),
            ).start()

    def z_sem(group, step, k, j):
        return r_z.at[step * 4 + k * 2 + j if group == 0 else 8 + group * 8 + step * 2 + k]

    z_bytes = zrecv.at[0, 0, pl.ds(0, 2), rows_of(0)]

    def zsum(group, step, k, j):
        rows = rows_of(group)
        slots = 1 if group == 0 else 2
        adds = step > 1 or (step == 1 and k == 1)
        if adds:
            wait_bytes(z_bytes, z_sem(group, step - 1, k, j))
        for way in range(2):
            first = 2 * (way if k == 1 else 1 - way) + j
            for slot in range(first, first + slots):
                own = branch(group, ring(z, 4 - step if way == 0 else 4 + step), slot)
                if adds:
                    own = (own.astype(F32) + zrecv[way, step - 1, slot, rows].astype(F32)).astype(BF16)
                zsend[way, step, slot, rows] = own
            part = pl.ds(first, slots)
            remote(
                zsend.at[way, step, part, rows], zrecv.at[way, step, part, rows], s_z, z_sem(group, step, k, j),
                z_dev(1 if way == 0 else 7),
            ).start()

    x_section = z * 2 + xl
    x_source = xh * 2 + c

    def zlast(group):
        rows = rows_of(group)
        for k in range(2):
            for j in range(2 if group == 0 else 1):
                wait_bytes(z_bytes, z_sem(group, 3, k, j))

        def one(slot, carry):
            total = branch(group, z, slot).astype(F32)
            total = total + (zrecv[0, 3, slot, rows].astype(F32) + zrecv[1, 3, slot, rows].astype(F32))
            xsend[slot, rows] = total.astype(BF16)
            return carry

        lax.fori_loop(0, 4, one, 0)
        for slot in range(4):
            stays = jnp.logical_and(xh == xl, q == slot)

            @pl.when(stays)
            def _():
                pltpu.make_async_copy(xsend.at[slot, rows], xrecv.at[x_source, rows], r_x.at[group]).start()

            @pl.when(jnp.logical_not(stays))
            def _():
                remote(
                    xsend.at[slot, rows], xrecv.at[x_source, rows], s_x, r_x.at[group], (x_section, y * 4 + slot)
                ).start()

    ended = {"adam": 0}

    def xlast(group):
        rows = rows_of(group)
        wait_bytes(xrecv.at[:, rows], r_x.at[group])
        for col in range(2):
            total = xrecv[col, rows].astype(F32) + xrecv[2 + col, rows].astype(F32)
            o_in[rows, col * W : (col + 1) * W] = total.astype(BF16)

    def adam(half):
        for k in range(2):
            wait_bytes(yrecv.at[0, 0, part_rows(0)], r_y.at[half, 3, k])
        ended["adam"] += 1
        if ended["adam"] == 1:
            for load in loads[4:]:
                load.wait()
        rows = part_rows(half)
        cols = slice(half * 128, half * 128 + 128)
        gradient = jnp.transpose(gsum[y, rows] + (yrecv[0, 3, rows].astype(F32) + yrecv[1, 3, rows].astype(F32)))
        was = mas_v[:, cols]
        first_new = BETA_ONE * m1_v[:, cols] + (1.0 - BETA_ONE) * gradient
        second_new = BETA_TWO * m2_v[:, cols] + (1.0 - BETA_TWO) * gradient * gradient
        direction = (
            first_new / (1.0 - BETA_ONE**STEP) / (jnp.sqrt(second_new / (1.0 - BETA_TWO**STEP)) + ADAM_EPS)
        )
        updated = was - LEARN_RATE * (direction + DECAY_RATE * was)
        wn[y, half] = updated.astype(BF16)
        for k in range(2):
            gather_send(wn.at[:, half], s_n, r_n.at[half], 0, k)
        o_master[0, :, cols] = updated
        o_m1[0, :, cols] = first_new
        o_m2[0, :, cols] = second_new

    def next(half, off):
        block = ring(y, off)
        part = jnp.dot(hid[block].reshape(4 * TOK, W), wn[block, half], preferred_element_type=F32)
        part = part.reshape(4, TOK, 128)
        kvn[half] = part if off == 0 else kvn[half] + part

    def share(half):
        remote(kvn.at[half, mates[2]], knc.at[half], s_kc, r_kc.at[half], mate_dev(mates[0])).start()
        remote(kvn.at[half, mates[0]], knr.at[half], s_kc, r_k.at[half], mate_dev(mates[0])).start()

    def cross(half):
        wait_bytes(knc.at[half], r_kc.at[half])
        kvs[half] = (kvn[half, mates[1]] + knc[half]).astype(BF16)
        remote(kvs.at[half], kns.at[half], s_k, r_k.at[half], mate_dev(mates[1])).start()

    def finish(half):
        wait_bytes(xa.at[0, pl.ds(0, 3), rows_of(0)], r_k.at[half])
        total = (kvn[half, q] + knr[half]) + kns[half].astype(F32)
        o_kv[0, :, half * 128 : half * 128 + 128] = total

    takes = {
        "relay": relay, "prepare": prepare, "old": old, "new": new, "arrive": arrive, "back": back, "grad": grad,
        "put": put, "get": get, "ysum": ysum, "zsum": zsum, "zlast": zlast, "xlast": xlast, "adam": adam,
        "next": next, "share": share, "cross": cross, "finish": finish,
    }
    for name, *where in STEPS:
        with part_of(name + "_".join(str(n) for n in where)):
            takes[name](*where)

    with part_of("sent"):
        wait_bytes(xa.at[pl.ds(0, 6)], s_acts)
        wait_bytes(kvb.at[pl.ds(0, 3)], s_kv)
        wait_bytes(rmb.at[pl.ds(0, 3)], s_rm)
        wait_bytes(mrecv, s_m)
        wait_bytes(wt.at[pl.ds(0, 7)], s_w)
        wait_bytes(wn.at[pl.ds(0, 7)], s_n)
        wait_bytes(wt.at[pl.ds(0, 7)], s_y)
        wait_bytes(hid.at[pl.ds(0, 7)], s_z)
        wait_bytes(kvn.at[0], s_kc)
        wait_bytes(kvs, s_k)

        @pl.when(xh == xl)
        def _():
            wait_bytes(xsend.at[pl.ds(0, 3)], s_x)

        @pl.when(xh != xl)
        def _():
            wait_bytes(xsend, s_x)


def write_out(*refs):
    sources, targets, done = refs[:5], refs[5:10], refs[10]
    copies = [pltpu.make_async_copy(sources[i], targets[i], done.at[i]) for i in range(5)]
    for copy in copies:
        copy.start()
    for copy in copies:
        copy.wait()


def per_device(acts, gain, kv_grad, master, moment_one, moment_two):
    anywhere = pl.BlockSpec(memory_space=pl.ANY)
    vmem = pltpu.VMEM
    dma = pltpu.SemaphoreType.DMA
    rows = jax.ShapeDtypeStruct((1, W, W), F32)
    scratch = [
        vmem((TOK, D), BF16),
        vmem((1, D), F32),
        vmem((W, W), F32), vmem((W, W), F32), vmem((W, W), F32),
        vmem((N, 4, TOK, W), BF16),
        vmem((4, TOK, W), BF16),
        vmem((4, W, TOK), BF16),
        vmem((4, 8, 128), F32),
        vmem((4, TOK, 128), F32),
        vmem((N, W, W), BF16), vmem((N, 2, W, 128), BF16),
        vmem((N, 4, TOK, W), BF16),
        vmem((N, 4, TOK, W), F32),
        vmem((4, TOK, 128), F32),
        vmem((len(GROUPS), 8, 128), F32),
        vmem((len(GROUPS), 3, 8, 128), F32),
        vmem((4, TOK, 128), F32),
        vmem((N, W, W), F32),
        vmem((2, 4, W, W), BF16), vmem((2, 4, W, W), BF16),
        vmem((2, 4, 4, TOK, W), BF16), vmem((2, 4, 4, TOK, W), BF16),
        vmem((4, TOK, W), BF16), vmem((4, TOK, W), BF16),
        vmem((2, 4, TOK, 128), F32), vmem((2, TOK, 128), BF16),
        vmem((2, TOK, 128), F32), vmem((2, TOK, 128), F32), vmem((2, TOK, 128), BF16),
        dma((6,)), dma,
        dma, dma, dma, dma, dma, dma, dma, dma, dma, dma, dma,
        dma((len(SETS),)), dma((3,)), dma, dma((len(GROUPS),)),
        dma((4, 2)), dma((2, 4, 2)), dma((2, 4, 2)), dma((32,)),
        dma((len(GROUPS),)), dma((2,)), dma((2,)),
    ]
    shapes = (
        rows, rows, rows,
        jax.ShapeDtypeStruct((TOK, 2 * W), BF16),
        jax.ShapeDtypeStruct((1, TOK, W), F32),
    )
    given = [
        pltpu.with_memory_space_constraint(a, pltpu.HBM)
        for a in (acts, gain, kv_grad, master, moment_one, moment_two)
    ]
    results = pl.pallas_call(
        kernel,
        out_shape=tuple(vmem(shape.shape, shape.dtype) for shape in shapes),
        in_specs=[pl.BlockSpec(memory_space=pltpu.HBM)] * 6,
        out_specs=(pl.BlockSpec(memory_space=pltpu.VMEM),) * 5,
        scratch_shapes=scratch,
        compiler_params=pltpu.CompilerParams(
            collective_id=0, has_side_effects=True, vmem_limit_bytes=VMEM_BYTES
        ),
        cost_estimate=pl.CostEstimate(flops=1_700_000_000, bytes_accessed=6_000_000, transcendentals=200_000),
    )(*given)
    return pl.pallas_call(
        write_out,
        out_shape=shapes,
        in_specs=[pl.BlockSpec(memory_space=pltpu.VMEM)] * 5,
        out_specs=(anywhere,) * 5,
        scratch_shapes=[dma((5,))],
        cost_estimate=pl.CostEstimate(flops=0, bytes_accessed=2_100_000, transcendentals=0),
    )(*[pltpu.with_memory_space_constraint(a, pltpu.VMEM) for a in results])


def solution(mesh):
    placed = (
        P("section", "dp", None),
        P("section", None),
        P("section", "dp", None),
        P("section", "dp", None),
        P("section", "dp", None),
        P("section", "dp", None),
    )
    return jax.shard_map(
        per_device,
        mesh=mesh,
        in_specs=placed,
        out_specs=(
            P("section", "dp", None),
            P("section", "dp", None),
            P("section", "dp", None),
            P("dp", "section"),
            P("section", "dp", None),
        ),
        check_vma=False,
    )
```

time: 300 us -> 71 us (0.24)
  waiting for transfers between devices: 203 us -> 0 us
  Pallas kernels: 0 us -> 70.2 us
  blocking collectives: 60.8 us -> 0 us
  between operations: 13.8 us -> 0.64 us
  matrix products: 12.5 us -> 0 us
  other arithmetic: 8.26 us -> 0 us
    reduce_scatter x1 -> x0, waiting for transfers between devices: 127 us -> none  [per_device(): lax.psum_scatter(lax.dot_general(hidden, upstream, (((0,), (0,)), ((), ()...]
    all_gather x2 -> x0, waiting for transfers between devices: 76.3 us -> none  [the longest x1 71.3 us: per_device(): lax.all_gather(owned_rows.astype(jnp.bfloat16), 'dp', axis=0, tiled=True)]
    pallas_call x0 -> x2, Pallas kernels: none -> 70.2 us  [the longest x1 69.2 us: per_device(): pl.pallas_call(kernel, out_shape=tuple((vmem(shape.shape, shape.dtype) fo...]
    all_to_all x1 -> x0, blocking collectives: 60.8 us -> none  [per_device(): lax.all_to_all(column_blocks, 'section', split_axis=1, concat_axis=1, til...]
    dot_general x3 -> x0, matrix products: 12.5 us -> none  [the longest x1 4.99 us: per_device(): lax.dot_general(hidden, upstream, (((0,), (0,)), ((), ())), preferred_ele...]
    reduce_sum x2 -> x0, other arithmetic: 4.66 us -> none  [the longest x1 2.58 us: per_device(): jnp.sum(received, axis=1, dtype=jnp.float32).astype(jnp.bfloat16)]
    convert_element_type x3 -> x0, other arithmetic: 3.59 us -> none  [the longest x1 2.02 us: per_device(): fresh_part = updated.astype(jnp.bfloat16)]
  transfers between devices with their start and end apart: 3 -> 0, of which waited for: 3 -> 0; matrix products, arithmetic and copies ran while one was open for 3% -> 0% of each run, Pallas kernels for 0% -> 0%
where the time goes in v3:
time: 71 us; the launch traced here: 70.8 us
  Pallas kernels  70.2 us (99%)
    pallas_call x1, Pallas kernels, per_device(): pl.pallas_call(kernel, out_shape=tuple((vmem(shape.shape, shape.dtype) fo...  69.2 us

profile of v3, /device:TPU:1, one launch (start us, length us, event | category | flops | bytes accessed | tf_op | source)
XLA Modules:
  0.0 70.8 jit_solution(7573323008398741927)
XLA Ops:
  0.6 69.2 %shard_map.101 = (f32[1,256,256]{2,1,0:T(8,128)S(1)}, f32[1,256,256]{2,1,0:T(8,128)S(1)}, f32[1,256,256]{2,1,0:T(8,128)S(1)}, bf16[128,512]{1,0:T(8,128)(2,1)S(1)}, f32[1,128,256]{2,1,0:T(8,128)S(1)}) custom-call(bf16[1,128,8192]{2,1,0:T(8,128)(2,1)} %acts.1, f32[1,8192]{1,0:T(1,128)} %gain.1, bf16[1,128,256]{2,1,0:T(8,128)(2,1)} %kv.1, ...), custom_call_target="tpu_custom_call" | custom-call | flops 1700000000 | bytes 6000000 | tf_op jit(solution)/shard_map/pallas_call | solution.py:504
  69.8 1.0 %shard_map.102 = (f32[1,256,256]{2,1,0:T(8,128)}, f32[1,256,256]{2,1,0:T(8,128)}, f32[1,256,256]{2,1,0:T(8,128)}, bf16[128,512]{1,0:T(8,128)(2,1)}, f32[1,128,256]{2,1,0:T(8,128)}) custom-call(f32[1,256,256]{2,1,0:T(8,128)S(1)} %get-tuple-element.10.refs_0_, f32[1,256,256]{2,1,0:T(8,128)S(1)} %get-tuple-element.11.refs_1_, ...), custom_call_target="tpu_custom_call" | custom-call | bytes 2100000 | tf_op jit(solution)/shard_map/pallas_call | solution.py:515

commit v4 on v3

--- a/solution.py
+++ b/solution.py
@@ -25,38 +25,37 @@
 VMEM_BYTES = 48 * 1024 * 1024
 GROUPS = ((0, 64), (64, 32), (96, 32))
 SETS = (
-    (0, 0), (0, 7), (0, 1), (0, 2), (0, 6), (0, 5), (0, 3), (0, 4),
-    (1, 4), (2, 4), (1, 3), (2, 3), (1, 5), (2, 5), (1, 2), (1, 6),
-    (2, 6), (2, 2), (1, 7), (2, 7), (1, 1), (2, 1), (1, 0), (2, 0),
+    (0, 0), (0, 4), (0, 7), (0, 1), (0, 5), (0, 3), (0, 2), (0, 6),
+    (1, 4), (2, 4), (1, 3), (2, 3), (1, 5), (2, 5), (1, 6), (2, 6),
+    (1, 2), (2, 2), (1, 7), (2, 7), (1, 1), (2, 1), (1, 0), (2, 0),
 )
-AHEAD = 5
+AHEAD = 7
 HOLD = 24
 STEPS = (
-    ("relay",), ("old", 1, 0), ("old", 1, 1), ("prepare",), ("arrive", 0), ("arrive", 1), ("back", 0, 0),
-    ("back", 0, 7), ("old", 2, 0), ("arrive", 2), ("back", 0, 1), ("old", 2, 1), ("arrive", 3), ("back", 0, 2),
-    ("arrive", 4), ("back", 0, 6), ("old", 3, 0), ("arrive", 5), ("old", 3, 1), ("back", 0, 5), ("arrive", 6),
-    ("back", 0, 3), ("old", 4, 0), ("arrive", 7), ("back", 0, 4), ("put", 0), ("arrive", 8), ("back", 1, 4),
-    ("arrive", 9), ("grad", 4), ("ysum", 0, 0, 1), ("ysum", 1, 0, 1), ("back", 2, 4), ("arrive", 10), ("back", 1, 3),
-    ("arrive", 11), ("grad", 3), ("back", 2, 3), ("arrive", 12), ("get", 0), ("zsum", 0, 0, 1, 0),
-    ("zsum", 0, 1, 0, 0), ("zsum", 0, 0, 1, 1), ("zsum", 0, 1, 0, 1), ("back", 1, 5), ("arrive", 13), ("grad", 5),
-    ("ysum", 0, 1, 0), ("ysum", 0, 1, 1), ("ysum", 1, 1, 0), ("back", 2, 5), ("arrive", 14), ("back", 1, 2),
-    ("ysum", 1, 1, 1), ("arrive", 15), ("back", 1, 6), ("arrive", 16), ("grad", 6), ("zsum", 0, 1, 1, 0),
-    ("back", 2, 6), ("arrive", 17), ("grad", 2), ("zsum", 0, 2, 0, 0), ("ysum", 0, 2, 0), ("back", 2, 2),
-    ("arrive", 18), ("back", 1, 7), ("zsum", 0, 1, 1, 1), ("ysum", 0, 2, 1), ("arrive", 19), ("grad", 7),
-    ("zsum", 0, 2, 0, 1), ("ysum", 1, 2, 0), ("back", 2, 7), ("arrive", 20), ("back", 1, 1), ("zsum", 0, 2, 1, 0),
-    ("ysum", 1, 2, 1), ("arrive", 21), ("grad", 1), ("zsum", 0, 3, 0, 0), ("ysum", 0, 3, 0), ("back", 2, 1),
-    ("arrive", 22), ("back", 1, 0), ("put", 1), ("zsum", 0, 2, 1, 1), ("ysum", 0, 3, 1), ("arrive", 23), ("grad", 0),
-    ("back", 2, 0), ("put", 2), ("zsum", 0, 3, 0, 1), ("ysum", 1, 3, 0), ("zsum", 0, 3, 1, 0), ("ysum", 1, 3, 1),
-    ("get", 1), ("zsum", 1, 0, 1, 0), ("zsum", 1, 1, 0, 0), ("get", 2), ("adam", 0), ("zsum", 2, 0, 1, 0),
-    ("zsum", 2, 1, 0, 0), ("zsum", 0, 3, 1, 1), ("next", 0, 0), ("adam", 1), ("next", 1, 0), ("zsum", 1, 1, 1, 0),
-    ("zsum", 1, 2, 0, 0), ("new", 0, 1, 0), ("zsum", 2, 1, 1, 0), ("new", 0, 1, 1), ("next", 0, 1), ("next", 0, 7),
-    ("zsum", 2, 2, 0, 0), ("new", 1, 1, 0), ("zlast", 0), ("new", 1, 1, 1), ("next", 1, 1), ("next", 1, 7),
-    ("zsum", 1, 2, 1, 0), ("new", 0, 2, 0), ("zsum", 1, 3, 0, 0), ("new", 0, 2, 1), ("next", 0, 2), ("next", 0, 6),
-    ("zsum", 2, 2, 1, 0), ("new", 1, 2, 0), ("zsum", 2, 3, 0, 0), ("new", 1, 2, 1), ("next", 1, 2), ("next", 1, 6),
-    ("zsum", 1, 3, 1, 0), ("new", 0, 3, 0), ("new", 0, 3, 1), ("next", 0, 3), ("next", 0, 5), ("zsum", 2, 3, 1, 0),
-    ("new", 1, 3, 0), ("xlast", 0), ("new", 1, 3, 1), ("next", 1, 3), ("next", 1, 5), ("zlast", 1), ("new", 0, 4, 0),
-    ("next", 0, 4), ("share", 0), ("zlast", 2), ("new", 1, 4, 0), ("next", 1, 4), ("share", 1), ("cross", 0),
-    ("cross", 1), ("xlast", 1), ("finish", 0), ("xlast", 2), ("finish", 1),
+    ("relay",), ("old", 1, 0), ("old", 1, 1), ("prepare",), ("project", 0), ("project", 1), ("project", 7),
+    ("arrive", 0), ("back", 0, 0), ("arrive", 1), ("arrive", 2), ("old", 2, 0), ("back", 0, 7), ("arrive", 3),
+    ("back", 0, 1), ("old", 2, 1), ("project", 2), ("project", 6), ("arrive", 4), ("arrive", 5), ("old", 3, 0),
+    ("arrive", 6), ("back", 0, 2), ("old", 3, 1), ("project", 3), ("back", 0, 3), ("project", 5), ("back", 0, 5),
+    ("arrive", 7), ("back", 0, 6), ("old", 4, 0), ("project", 4), ("back", 0, 4), ("put", 0), ("arrive", 10),
+    ("arrive", 8), ("arrive", 9), ("grad", 4), ("ysum", 0, 0, 1), ("ysum", 1, 0, 1), ("arrive", 11), ("grad", 3),
+    ("arrive", 12), ("arrive", 13), ("grad", 5), ("ysum", 0, 1, 0), ("ysum", 1, 1, 0), ("arrive", 14), ("get", 0),
+    ("zsum", 0, 0, 1, 0), ("zsum", 0, 0, 1, 1), ("zsum", 0, 1, 0, 0), ("zsum", 0, 1, 0, 1), ("arrive", 15),
+    ("grad", 6), ("ysum", 0, 1, 1), ("arrive", 16), ("ysum", 1, 1, 1), ("arrive", 17), ("grad", 2), ("arrive", 18),
+    ("ysum", 0, 2, 0), ("zsum", 0, 1, 1, 0), ("arrive", 19), ("grad", 7), ("ysum", 1, 2, 0), ("zsum", 0, 1, 1, 1),
+    ("arrive", 20), ("ysum", 0, 2, 1), ("zsum", 0, 2, 0, 0), ("arrive", 21), ("grad", 1), ("ysum", 1, 2, 1),
+    ("zsum", 0, 2, 0, 1), ("arrive", 22), ("put", 1), ("ysum", 0, 3, 0), ("arrive", 23), ("put", 2), ("grad", 0),
+    ("zsum", 0, 2, 1, 0), ("ysum", 1, 3, 0), ("zsum", 0, 2, 1, 1), ("ysum", 0, 3, 1), ("get", 1),
+    ("zsum", 1, 0, 1, 0), ("zsum", 1, 1, 0, 0), ("zsum", 0, 3, 0, 0), ("ysum", 1, 3, 1), ("get", 2),
+    ("zsum", 2, 0, 1, 0), ("zsum", 2, 1, 0, 0), ("zsum", 0, 3, 0, 1), ("zsum", 0, 3, 1, 0), ("adam", 0),
+    ("next", 0, 0), ("zsum", 1, 1, 1, 0), ("adam", 1), ("next", 1, 0), ("zsum", 1, 2, 0, 0), ("zsum", 0, 3, 1, 1),
+    ("zsum", 2, 1, 1, 0), ("new", 0, 1, 0), ("zsum", 2, 2, 0, 0), ("new", 0, 1, 1), ("next", 0, 1), ("next", 0, 7),
+    ("new", 1, 1, 0), ("new", 1, 1, 1), ("next", 1, 1), ("next", 1, 7), ("zsum", 1, 2, 1, 0), ("new", 0, 2, 0),
+    ("zlast", 0), ("zsum", 1, 3, 0, 0), ("new", 0, 2, 1), ("next", 0, 2), ("next", 0, 6), ("zsum", 2, 2, 1, 0),
+    ("new", 1, 2, 0), ("zsum", 2, 3, 0, 0), ("new", 1, 2, 1), ("next", 1, 2), ("next", 1, 6), ("zsum", 1, 3, 1, 0),
+    ("new", 0, 3, 0), ("new", 0, 3, 1), ("next", 0, 3), ("next", 0, 5), ("zsum", 2, 3, 1, 0), ("new", 1, 3, 0),
+    ("new", 1, 3, 1), ("next", 1, 3), ("next", 1, 5), ("xlast", 0), ("zlast", 1), ("new", 0, 4, 0), ("next", 0, 4),
+    ("share", 0), ("cross", 0), ("new", 1, 4, 0), ("next", 1, 4), ("share", 1), ("zlast", 2), ("cross", 1),
+    ("xlast", 1), ("finish", 0), ("xlast", 2), ("finish", 1),
 )
 
 def part_of(name):
@@ -214,10 +213,11 @@
         def one(slot, carry):
             root = jnp.transpose(jnp.broadcast_to(rmb[slot][0:1, :], (128, 128)))
             invc[slot] = 1.0 / root
-            kvt[slot] = jnp.transpose(kvb[slot].astype(F32)).astype(BF16)
             return carry
 
         lax.fori_loop(0, 4, one, 0)
+        for slot in range(4):
+            kvt[:, slot * TOK : (slot + 1) * TOK] = jnp.transpose(kvb[slot].astype(F32)).astype(BF16)
 
     def old(hop, k):
         gather_step(wt, s_w, r_w, hop, k)
@@ -231,46 +231,46 @@
             sent[0] = later + 1
         sent[2] = k
 
+    def project(off):
+        block = ring(y, off)
+        product = jnp.dot(kvb[...].reshape(4 * TOK, W), wt[block], preferred_element_type=F32)
+        sc[block] = (product * gain_v[:, columns(block)]).reshape(4, TOK, W)
+        projected.add(off)
+
+    projected = set()
+    hidden_only = set()
+
+    def features(group, off, hides, means):
+        rows = rows_of(group)
+        block = ring(y, off)
+        gain_row = gain_v[:, columns(block)]
+
+        def one(slot, carry):
+            unit = xa[block, slot, rows, :].astype(F32) * wide(invc[slot, rows, :])
+            if hides:
+                hid[block, slot, rows, :] = (unit * gain_row).astype(BF16)
+            if means:
+                both = sc[block, slot, rows, :] * unit
+                macc[slot, rows, :] += both[:, :128] + both[:, 128:]
+            return carry
+
+        lax.fori_loop(0, 4, one, 0)
+
     def arrive(k):
         group, off = SETS[k]
-        rows = rows_of(group)
-        wait_bytes(xa.at[0, pl.ds(0, 3), rows], r_acts.at[k])
+        wait_bytes(xa.at[0, pl.ds(0, 3), rows_of(group)], r_acts.at[k])
         feed(k)
-        block = ring(y, off)
-        gain_row = gain_v[:, columns(block)]
-
-        def one(slot, carry):
-            unit = xa[block, slot, rows, :].astype(F32) * wide(invc[slot, rows, :])
-            hid[block, slot, rows, :] = (unit * gain_row).astype(BF16)
-            return carry
-
-        lax.fori_loop(0, 4, one, 0)
+        features(group, off, True, off in projected)
+        if off not in projected:
+            hidden_only.add((group, off))
 
     def back(group, off):
-        rows = rows_of(group)
-        count = GROUPS[group][1]
-        block = ring(y, off)
-        gain_row = gain_v[:, columns(block)]
-        product = jnp.dot(kvb[:, rows, :].reshape(4 * count, W), wt[block], preferred_element_type=F32)
-        sc[block, :, rows, :] = product.reshape(4, count, W)
-
-        def one(slot, carry):
-            unit = xa[block, slot, rows, :].astype(F32) * wide(invc[slot, rows, :])
-            scaled = sc[block, slot, rows, :] * gain_row
-            sc[block, slot, rows, :] = scaled
-            both = scaled * unit
-            macc[slot, rows, :] += both[:, :128] + both[:, 128:]
-            return carry
-
-        lax.fori_loop(0, 4, one, 0)
+        if (group, off) in hidden_only:
+            features(group, off, False, True)
 
     def grad(off):
         block = ring(y, off)
-        total = None
-        for slot in range(4):
-            product = jnp.dot(kvt[slot], hid[block, slot], preferred_element_type=F32).astype(BF16).astype(F32)
-            total = product if total is None else total + product
-        gsum[block] = total
+        gsum[block] = jnp.dot(kvt[...], hid[block].reshape(4 * TOK, W), preferred_element_type=F32)
 
     def put(group):
         rows = rows_of(group)
@@ -421,7 +421,7 @@
         o_kv[0, :, half * 128 : half * 128 + 128] = total
 
     takes = {
-        "relay": relay, "prepare": prepare, "old": old, "new": new, "arrive": arrive, "back": back, "grad": grad,
+        "relay": relay, "prepare": prepare, "old": old, "new": new, "arrive": arrive, "back": back, "grad": grad, "project": project,
         "put": put, "get": get, "ysum": ysum, "zsum": zsum, "zlast": zlast, "xlast": xlast, "adam": adam,
         "next": next, "share": share, "cross": cross, "finish": finish,
     }
@@ -470,7 +470,7 @@
         vmem((W, W), F32), vmem((W, W), F32), vmem((W, W), F32),
         vmem((N, 4, TOK, W), BF16),
         vmem((4, TOK, W), BF16),
-        vmem((4, W, TOK), BF16),
+        vmem((W, 4 * TOK), BF16),
         vmem((4, 8, 128), F32),
         vmem((4, TOK, 128), F32),
         vmem((N, W, W), BF16), vmem((N, 2, W, 128), BF16),

time: 71 us -> 68.8 us (0.969)
  Pallas kernels: 70.2 us -> 68 us
    pallas_call x1, Pallas kernels: 69.2 us -> 67 us  [per_device(): pl.pallas_call(kernel, out_shape=tuple((vmem(shape.shape, shape.dtype) fo...]
where the time goes in v4:
time: 68.8 us; the launch traced here: 68.7 us
  Pallas kernels  68 us (99%)
    pallas_call x1, Pallas kernels, per_device(): pl.pallas_call(kernel, out_shape=tuple((vmem(shape.shape, shape.dtype) fo...  67 us

profile of v4, /device:TPU:1, one launch (start us, length us, event | category | flops | bytes accessed | tf_op | source)
XLA Modules:
  0.0 68.7 jit_solution(14917398964298879922)
XLA Ops:
  0.6 67.0 %shard_map.101 = (f32[1,256,256]{2,1,0:T(8,128)S(1)}, f32[1,256,256]{2,1,0:T(8,128)S(1)}, f32[1,256,256]{2,1,0:T(8,128)S(1)}, bf16[128,512]{1,0:T(8,128)(2,1)S(1)}, f32[1,128,256]{2,1,0:T(8,128)S(1)}) custom-call(bf16[1,128,8192]{2,1,0:T(8,128)(2,1)} %acts.1, f32[1,8192]{1,0:T(1,128)} %gain.1, bf16[1,128,256]{2,1,0:T(8,128)(2,1)} %kv.1, ...), custom_call_target="tpu_custom_call" | custom-call | flops 1700000000 | bytes 6000000 | tf_op jit(solution)/shard_map/pallas_call | solution.py:504
  67.7 1.0 %shard_map.102 = (f32[1,256,256]{2,1,0:T(8,128)}, f32[1,256,256]{2,1,0:T(8,128)}, f32[1,256,256]{2,1,0:T(8,128)}, bf16[128,512]{1,0:T(8,128)(2,1)}, f32[1,128,256]{2,1,0:T(8,128)}) custom-call(f32[1,256,256]{2,1,0:T(8,128)S(1)} %get-tuple-element.10.refs_0_, f32[1,256,256]{2,1,0:T(8,128)S(1)} %get-tuple-element.11.refs_1_, ...), custom_call_target="tpu_custom_call" | custom-call | bytes 2100000 | tf_op jit(solution)/shard_map/pallas_call | solution.py:515

commit v5 on v4

--- a/solution.py
+++ b/solution.py
@@ -25,37 +25,40 @@
 VMEM_BYTES = 48 * 1024 * 1024
 GROUPS = ((0, 64), (64, 32), (96, 32))
 SETS = (
-    (0, 0), (0, 4), (0, 7), (0, 1), (0, 5), (0, 3), (0, 2), (0, 6),
-    (1, 4), (2, 4), (1, 3), (2, 3), (1, 5), (2, 5), (1, 6), (2, 6),
-    (1, 2), (2, 2), (1, 7), (2, 7), (1, 1), (2, 1), (1, 0), (2, 0),
+    (0, 0), (0, 7), (0, 1), (0, 2), (0, 6), (0, 5), (0, 3), (0, 4),
+    (1, 4), (2, 4), (1, 3), (2, 3), (1, 5), (2, 5), (1, 2), (1, 6),
+    (2, 6), (2, 2), (1, 7), (2, 7), (1, 1), (2, 1), (1, 0), (2, 0),
 )
-AHEAD = 7
+AHEAD = 5
 HOLD = 24
 STEPS = (
-    ("relay",), ("old", 1, 0), ("old", 1, 1), ("prepare",), ("project", 0), ("project", 1), ("project", 7),
-    ("arrive", 0), ("back", 0, 0), ("arrive", 1), ("arrive", 2), ("old", 2, 0), ("back", 0, 7), ("arrive", 3),
-    ("back", 0, 1), ("old", 2, 1), ("project", 2), ("project", 6), ("arrive", 4), ("arrive", 5), ("old", 3, 0),
-    ("arrive", 6), ("back", 0, 2), ("old", 3, 1), ("project", 3), ("back", 0, 3), ("project", 5), ("back", 0, 5),
-    ("arrive", 7), ("back", 0, 6), ("old", 4, 0), ("project", 4), ("back", 0, 4), ("put", 0), ("arrive", 10),
-    ("arrive", 8), ("arrive", 9), ("grad", 4), ("ysum", 0, 0, 1), ("ysum", 1, 0, 1), ("arrive", 11), ("grad", 3),
-    ("arrive", 12), ("arrive", 13), ("grad", 5), ("ysum", 0, 1, 0), ("ysum", 1, 1, 0), ("arrive", 14), ("get", 0),
-    ("zsum", 0, 0, 1, 0), ("zsum", 0, 0, 1, 1), ("zsum", 0, 1, 0, 0), ("zsum", 0, 1, 0, 1), ("arrive", 15),
-    ("grad", 6), ("ysum", 0, 1, 1), ("arrive", 16), ("ysum", 1, 1, 1), ("arrive", 17), ("grad", 2), ("arrive", 18),
-    ("ysum", 0, 2, 0), ("zsum", 0, 1, 1, 0), ("arrive", 19), ("grad", 7), ("ysum", 1, 2, 0), ("zsum", 0, 1, 1, 1),
-    ("arrive", 20), ("ysum", 0, 2, 1), ("zsum", 0, 2, 0, 0), ("arrive", 21), ("grad", 1), ("ysum", 1, 2, 1),
-    ("zsum", 0, 2, 0, 1), ("arrive", 22), ("put", 1), ("ysum", 0, 3, 0), ("arrive", 23), ("put", 2), ("grad", 0),
-    ("zsum", 0, 2, 1, 0), ("ysum", 1, 3, 0), ("zsum", 0, 2, 1, 1), ("ysum", 0, 3, 1), ("get", 1),
-    ("zsum", 1, 0, 1, 0), ("zsum", 1, 1, 0, 0), ("zsum", 0, 3, 0, 0), ("ysum", 1, 3, 1), ("get", 2),
-    ("zsum", 2, 0, 1, 0), ("zsum", 2, 1, 0, 0), ("zsum", 0, 3, 0, 1), ("zsum", 0, 3, 1, 0), ("adam", 0),
-    ("next", 0, 0), ("zsum", 1, 1, 1, 0), ("adam", 1), ("next", 1, 0), ("zsum", 1, 2, 0, 0), ("zsum", 0, 3, 1, 1),
-    ("zsum", 2, 1, 1, 0), ("new", 0, 1, 0), ("zsum", 2, 2, 0, 0), ("new", 0, 1, 1), ("next", 0, 1), ("next", 0, 7),
-    ("new", 1, 1, 0), ("new", 1, 1, 1), ("next", 1, 1), ("next", 1, 7), ("zsum", 1, 2, 1, 0), ("new", 0, 2, 0),
-    ("zlast", 0), ("zsum", 1, 3, 0, 0), ("new", 0, 2, 1), ("next", 0, 2), ("next", 0, 6), ("zsum", 2, 2, 1, 0),
-    ("new", 1, 2, 0), ("zsum", 2, 3, 0, 0), ("new", 1, 2, 1), ("next", 1, 2), ("next", 1, 6), ("zsum", 1, 3, 1, 0),
-    ("new", 0, 3, 0), ("new", 0, 3, 1), ("next", 0, 3), ("next", 0, 5), ("zsum", 2, 3, 1, 0), ("new", 1, 3, 0),
-    ("new", 1, 3, 1), ("next", 1, 3), ("next", 1, 5), ("xlast", 0), ("zlast", 1), ("new", 0, 4, 0), ("next", 0, 4),
-    ("share", 0), ("cross", 0), ("new", 1, 4, 0), ("next", 1, 4), ("share", 1), ("zlast", 2), ("cross", 1),
-    ("xlast", 1), ("finish", 0), ("xlast", 2), ("finish", 1),
+    ("relay",), ("old", 1, 0), ("old", 1, 1), ("prepare",), ("arrive", 0), ("arrive", 1), ("project", 0),
+    ("back", 0, 0), ("project", 1), ("arrive", 2), ("back", 0, 1), ("old", 2, 0), ("project", 7), ("back", 0, 7),
+    ("arrive", 3), ("old", 2, 1), ("project", 2), ("back", 0, 2), ("project", 6), ("arrive", 4), ("back", 0, 6),
+    ("arrive", 5), ("old", 3, 0), ("arrive", 6), ("old", 3, 1), ("project", 3), ("back", 0, 3), ("project", 5),
+    ("back", 0, 5), ("arrive", 7), ("arrive", 8), ("arrive", 9), ("grad", 4), ("ysum", 0, 0, 1), ("ysum", 1, 0, 1),
+    ("old", 4, 0), ("project", 4), ("back", 0, 4), ("put", 0), ("back", 1, 4), ("back", 2, 4), ("arrive", 10),
+    ("back", 1, 3), ("arrive", 11), ("back", 2, 3), ("grad", 3), ("arrive", 12), ("back", 1, 5), ("arrive", 13),
+    ("back", 2, 5), ("grad", 5), ("ysum", 0, 1, 0), ("ysum", 1, 1, 0), ("arrive", 14), ("ysum", 0, 1, 1),
+    ("back", 1, 2), ("get", 0), ("zsum", 0, 0, 1, 0), ("zsum", 0, 0, 1, 1), ("zsum", 0, 1, 0, 0),
+    ("zsum", 0, 1, 0, 1), ("ysum", 1, 1, 1), ("arrive", 15), ("back", 1, 6), ("arrive", 16), ("back", 2, 6),
+    ("grad", 6), ("arrive", 17), ("back", 2, 2), ("grad", 2), ("ysum", 0, 2, 0), ("arrive", 18), ("back", 1, 7),
+    ("zsum", 0, 1, 1, 0), ("ysum", 1, 2, 0), ("arrive", 19), ("back", 2, 7), ("grad", 7), ("zsum", 0, 1, 1, 1),
+    ("ysum", 0, 2, 1), ("arrive", 20), ("back", 1, 1), ("zsum", 0, 2, 0, 0), ("arrive", 21), ("ysum", 1, 2, 1),
+    ("back", 2, 1), ("grad", 1), ("zsum", 0, 2, 0, 1), ("arrive", 22), ("back", 1, 0), ("put", 1), ("ysum", 0, 3, 0),
+    ("arrive", 23), ("back", 2, 0), ("put", 2), ("grad", 0), ("ysum", 1, 3, 0), ("zsum", 0, 2, 1, 0),
+    ("ysum", 0, 3, 1), ("zsum", 0, 2, 1, 1), ("ysum", 1, 3, 1), ("zsum", 0, 3, 0, 0), ("get", 1),
+    ("zsum", 1, 0, 1, 0), ("zsum", 1, 1, 0, 0), ("zsum", 0, 3, 0, 1), ("get", 2), ("zsum", 2, 0, 1, 0),
+    ("zsum", 2, 1, 0, 0), ("zsum", 0, 3, 1, 0), ("adam", 0), ("next", 0, 0), ("adam", 1), ("next", 1, 0),
+    ("zsum", 1, 1, 1, 0), ("zsum", 0, 3, 1, 1), ("zsum", 1, 2, 0, 0), ("new", 0, 1, 0), ("zsum", 2, 1, 1, 0),
+    ("new", 0, 1, 1), ("next", 0, 1), ("next", 0, 7), ("zsum", 2, 2, 0, 0), ("new", 1, 1, 0), ("new", 1, 1, 1),
+    ("next", 1, 1), ("next", 1, 7), ("new", 0, 2, 0), ("zsum", 1, 2, 1, 0), ("zlast", 0), ("new", 0, 2, 1),
+    ("next", 0, 2), ("next", 0, 6), ("zsum", 1, 3, 0, 0), ("new", 1, 2, 0), ("zsum", 2, 2, 1, 0), ("new", 1, 2, 1),
+    ("next", 1, 2), ("next", 1, 6), ("zsum", 2, 3, 0, 0), ("new", 0, 3, 0), ("zsum", 1, 3, 1, 0), ("new", 0, 3, 1),
+    ("next", 0, 3), ("next", 0, 5), ("new", 1, 3, 0), ("zsum", 2, 3, 1, 0), ("xlast", 0), ("new", 1, 3, 1),
+    ("next", 1, 3), ("next", 1, 5), ("new", 0, 4, 0), ("next", 0, 4), ("share", 0), ("zlast", 1), ("cross", 0),
+    ("new", 1, 4, 0), ("next", 1, 4), ("share", 1), ("zlast", 2), ("cross", 1), ("xlast", 1), ("finish", 0),
+    ("xlast", 2), ("finish", 1),
 )
 
 def part_of(name):

time: 68.8 us -> 69.1 us (level)
  no operation moved by 1% of the time
where the time goes in v5:
time: 69.1 us; the launch traced here: 69 us
  Pallas kernels  68.4 us (99%)
    pallas_call x1, Pallas kernels, per_device(): pl.pallas_call(kernel, out_shape=tuple((vmem(shape.shape, shape.dtype) fo...  67.4 us

profile of v5, /device:TPU:1, one launch (start us, length us, event | category | flops | bytes accessed | tf_op | source)
XLA Modules:
  0.0 69.0 jit_solution(1329059616067922159)
XLA Ops:
  0.6 67.4 %shard_map.101 = (f32[1,256,256]{2,1,0:T(8,128)S(1)}, f32[1,256,256]{2,1,0:T(8,128)S(1)}, f32[1,256,256]{2,1,0:T(8,128)S(1)}, bf16[128,512]{1,0:T(8,128)(2,1)S(1)}, f32[1,128,256]{2,1,0:T(8,128)S(1)}) custom-call(bf16[1,128,8192]{2,1,0:T(8,128)(2,1)} %acts.1, f32[1,8192]{1,0:T(1,128)} %gain.1, bf16[1,128,256]{2,1,0:T(8,128)(2,1)} %kv.1, ...), custom_call_target="tpu_custom_call" | custom-call | flops 1700000000 | bytes 6000000 | tf_op jit(solution)/shard_map/pallas_call | solution.py:507
  68.0 1.0 %shard_map.102 = (f32[1,256,256]{2,1,0:T(8,128)}, f32[1,256,256]{2,1,0:T(8,128)}, f32[1,256,256]{2,1,0:T(8,128)}, bf16[128,512]{1,0:T(8,128)(2,1)}, f32[1,128,256]{2,1,0:T(8,128)}) custom-call(f32[1,256,256]{2,1,0:T(8,128)S(1)} %get-tuple-element.10.refs_0_, f32[1,256,256]{2,1,0:T(8,128)S(1)} %get-tuple-element.11.refs_1_, ...), custom_call_target="tpu_custom_call" | custom-call | bytes 2100000 | tf_op jit(solution)/shard_map/pallas_call | solution.py:518
